TPU v7x, 32 devices: a whole 2x2x4 slice. The times are simulated.
32 devices in a mesh: dp: 16 (over z, y, x), cores: 2 (over core).
Axes of the slice: x: 2, y: 2, z: 4, core: 2. Of those that a mesh axis runs over, the one named last changes fastest.
Arguments:
- queries: bfloat16 [16384, 1024], P(('dp', 'cores')), may hold values from -4 to 4
- passages: bfloat16 [16384, 1024], P(('dp', 'cores')), may hold values from -4 to 4
- positives: int32 [32, 512], P(('dp', 'cores')), may hold values from 0 to 511, each once within a row
- pair_blocks: int32 [32, 8], P(('dp', 'cores')), may hold values from 0 to 31, as said below
- negative_pair_count: int32 [32], P(('dp', 'cores')), may hold values from 1 to 8, as said below
Outputs:
- query_loss: float32 [32, 512], P(('dp', 'cores'))
- passage_loss: float32 [32, 512], P(('dp', 'cores'))
- query_grad: float32 [16384, 1024], P(('dp', 'cores'))
- passage_grad: float32 [16384, 1024], P(('dp', 'cores'))
Inputs may be any that keep to these rules, and one draw needn't show every extreme that they name: `pair_blocks`: row b lists 8 different blocks, each (b + o) mod 32 with 1 <= |o| <= 4, so every block within 4 of b in cyclic order appears once. `negative_pair_count`: some block has 8 hard negatives and some block has 1 in every draw.
All inputs are finite; a program needn't handle non-finite values.
Results may differ from a plain program's by a relative error of at most 0.0022.
Values may be sent and summed in bfloat16 or wider, within the bound.
A program may use at most 128 MiB of HBM per device.

v0:
```python
import jax
import jax.numpy as jnp
from jax import lax
from jax.sharding import PartitionSpec as P

RANGE = 4


logit_multiplier = 20.0
far_negative = -1e30


def shifted(value, axis, by):
    peers = lax.axis_size(axis)
    return lax.ppermute(value, axis, [(i, (i + by) % peers) for i in range(peers)])


def slot_offsets(reach):
    return [0] + [offset for offset in range(-reach, reach + 1) if offset != 0]


def slot_mask(pair_blocks, negative_pair_count, block_ids, blocks, reach):
    listed = pair_blocks.shape[1]
    used = jnp.arange(listed, dtype=jnp.int32)[None, :] < negative_pair_count[:, None]
    columns = []
    for offset in slot_offsets(reach):
        if offset == 0:
            columns.append(jnp.ones(block_ids.shape, dtype=bool))
        else:
            target = (block_ids + offset) % blocks
            columns.append(jnp.any((pair_blocks == target[:, None]) & used, axis=1))
    return jnp.stack(columns, axis=1)


def scores_of(query_rows, passage_rows):
    plain_similarities = lax.dot_general(
        query_rows, passage_rows, (((1,), (1,)), ((), ())), preferred_element_type=jnp.float32
    )
    return logit_multiplier * plain_similarities


def partial_stats(scores):
    row_top = jnp.max(scores, axis=1)
    line_exponential_sum = jnp.sum(jnp.exp(scores - row_top[:, None]), axis=1)
    col_top = jnp.max(scores, axis=0)
    col_total = jnp.sum(jnp.exp(scores - col_top[None, :]), axis=0)
    return (row_top, line_exponential_sum, col_top, col_total)


def merge_lse(tops, totals):
    top = jnp.max(tops, axis=0)
    return top + jnp.log(jnp.sum(totals * jnp.exp(tops - top), axis=0))


def weight_of(scores, row_lse, col_lse, present_markers, diagonal):
    similarity_gap = jnp.exp(scores - row_lse[:, None]) + jnp.exp(scores - col_lse[None, :])
    if diagonal is not None:
        similarity_gap = similarity_gap - 2.0 * diagonal
    return jnp.where(present_markers, logit_multiplier * similarity_gap, 0.0).astype(jnp.bfloat16)


def transposed_product(weight, rows):
    return lax.dot_general(
        weight, rows, (((0,), (0,)), ((), ())), preferred_element_type=jnp.float32
    )


def body(queries, passages, positives, pair_blocks, negative_pair_count):
    reach = RANGE
    blocks = lax.axis_size(("dp", "cores"))
    block = lax.axis_index(("dp", "cores"))
    offsets = slot_offsets(reach)
    mask = slot_mask(pair_blocks, negative_pair_count, block[None], blocks, reach)[0]
    width = passages.shape[0]
    columns = jnp.arange(width, dtype=jnp.int32)
    diagonal = (positives[0][:, None] == columns[None, :]).astype(jnp.float32)
    payload = passages[None]
    block_lookup = {0: payload}
    for offset in offsets[1:]:
        block_lookup[offset] = shifted(payload, ("dp", "cores"), -offset)
    own_scores = scores_of(queries, passages)
    row_pos = jnp.sum(own_scores * diagonal, axis=1)
    col_pos = jnp.sum(own_scores * diagonal, axis=0)
    tops, totals, col_tops, col_totals = ([], [], [], [])
    for slot, offset in enumerate(offsets):
        if offset == 0:
            stats = partial_stats(own_scores)
        else:

            def compute_stats(passage_rows=block_lookup[offset][0]):
                return partial_stats(scores_of(queries, passage_rows))

            stats = compute_stats()
        present_markers = mask[slot]
        tops.append(jnp.where(present_markers, stats[0], far_negative))
        totals.append(jnp.where(present_markers, stats[1], 0.0))
        col_tops.append(jnp.where(present_markers, stats[2], far_negative))
        col_totals.append(jnp.where(present_markers, stats[3], 0.0))
    row_lse = merge_lse(jnp.stack(tops), jnp.stack(totals))
    owner_tops = [col_tops[0]]
    owner_totals = [col_totals[0]]
    for slot in range(1, len(offsets)):
        got_top, got_total = shifted(
            (col_tops[slot], col_totals[slot]), ("dp", "cores"), offsets[slot]
        )
        owner_tops.append(got_top)
        owner_totals.append(got_total)
    col_lse = merge_lse(jnp.stack(owner_tops), jnp.stack(owner_totals))
    remote_lse = {0: col_lse}
    for offset in offsets[1:]:
        remote_lse[offset] = shifted(col_lse, ("dp", "cores"), -offset)
    query_grad = jnp.zeros(queries.shape, jnp.float32)
    passage_grad = jnp.zeros(passages.shape, jnp.float32)
    for slot, offset in enumerate(offsets):

        def make_terms(passage_rows=block_lookup[offset][0], offset=offset, slot=slot):
            scores = own_scores if offset == 0 else scores_of(queries, passage_rows)
            weight = weight_of(
                scores, row_lse, remote_lse[offset], mask[slot], diagonal if offset == 0 else None
            )
            return (weight, jnp.dot(weight, passage_rows, preferred_element_type=jnp.float32))

        weight, term = make_terms()
        query_grad = query_grad + term
        if offset == 0:
            passage_grad = transposed_product(weight, queries)
        else:
            partial_term = transposed_product(weight, queries)
            passage_grad = passage_grad + shifted(partial_term, ("dp", "cores"), offset)
    query_loss = (row_lse - row_pos)[None, :]
    passage_loss = (col_lse - col_pos)[None, :]
    return (query_loss, passage_loss, query_grad, passage_grad)


def solution(mesh):
    return jax.shard_map(
        body,
        mesh=mesh,
        in_specs=(
            P(("dp", "cores"), None),
            P(("dp", "cores"), None),
            P(("dp", "cores"), None),
            P(("dp", "cores"), None),
            P(("dp", "cores")),
        ),
        out_specs=(
            P(("dp", "cores"), None),
            P(("dp", "cores"), None),
            P(("dp", "cores"), None),
            P(("dp", "cores"), None),
        ),
        check_vma=False,
    )
```

profile of v0, /device:TPU:0, one launch (start us, length us, event | category | flops | bytes accessed | tf_op | source)
XLA Modules:
  0.0 567.5 jit_solution(10558664598975409957)
XLA Ops:
  0.7 6.1 %collective-permute-start.7 = (bf16[1,512,1024]{2,1,0:T(8,128)(2,1)}, bf16[1,512,1024]{2,1,0:T(8,128)(2,1)S(1)}, u32[]{:S(2)}, u32[]{:S(2)}) collective-permute-start(bf16[1,512,1024]{2,1,0:T(8,128)(2,1)} %bitcast.188), channel_id=1, source_target_pairs={{0,28},{1,29},{2,30},{3,31},{4,0},{5,1},{6,2},{7,3},{8,4},{9,5},{1... | collective-permute-start | bytes 3145736 | tf_op jit(solution)/shard_map/ppermute | solution.py:15
  7.4 3.8 collective-permute-start.6
  12.9 2.1 fusion.39
  15.7 0.8 and_reduce_fusion
  16.5 44.2 %collective-permute-done.7 = bf16[1,512,1024]{2,1,0:T(8,128)(2,1)S(1)} collective-permute-done((bf16[1,512,1024]{2,1,0:T(8,128)(2,1)}, bf16[1,512,1024]{2,1,0:T(8,128)(2,1)S(1)}, u32[]{:S(2)}, u32[]{:S(2)}) %collective-permute-start.7) | collective-permute-done | bytes 1048608 | tf_op jit(solution)/shard_map/ppermute | solution.py:15
  60.8 1.0 copy-done.1
  61.8 13.6 %collective-permute-start.4 = (bf16[1,512,1024]{2,1,0:T(8,128)(2,1)S(1)}, bf16[1,512,1024]{2,1,0:T(8,128)(2,1)S(1)}, u32[]{:S(2)}, u32[]{:S(2)}) collective-permute-start(bf16[1,512,1024]{2,1,0:T(8,128)(2,1)S(1)} %bitcast.193), channel_id=1, source_target_pairs={{0,31},{1,0},{2,1},{3,2},{4,3},{5,4},{6,5},{7,6},{8,7},{9,8},{10,9... | collective-permute-start | bytes 3145736 | tf_op jit(solution)/shard_map/ppermute | solution.py:15
  75.4 2.0 fusion.46
  77.6 2.0 fusion.40
  80.5 2.1 fusion.42
  82.9 2.1 fusion.45
  85.0 2.4 fusion.44
  87.4 32.6 %collective-permute-done.2 = bf16[1,512,1024]{2,1,0:T(8,128)(2,1)S(1)} collective-permute-done((bf16[1,512,1024]{2,1,0:T(8,128)(2,1)S(1)}, bf16[1,512,1024]{2,1,0:T(8,128)(2,1)S(1)}, u32[]{:S(2)}, u32[]{:S(2)}) %collective-permute-start.2) | collective-permute-done | bytes 1048608 | tf_op jit(solution)/shard_map/ppermute | solution.py:15
  120.0 0.8 fusion.41
  123.9 0.8 fusion.43
  125.8 0.7 broadcast_select_fusion.20
  127.7 0.8 fusion.38
  128.6 5.0 maximum_maximum_fusion.1
  134.0 1.2 broadcast_select_fusion.14
  135.2 1.3 broadcast_select_fusion.12
  136.5 1.2 broadcast_select_fusion.10
  137.7 1.3 broadcast_select_fusion.8
  139.2 3.9 collective-permute-start.14
  143.1 4.9 collective-permute-start.13
  148.6 4.6 collective-permute-start.16
  153.8 1.4 collective-permute-start.17
  158.6 1.2 collective-permute-start.19
  159.8 1.3 collective-permute-start.21
  161.1 2.1 collective-permute-start.22
  164.6 1.7 collective-permute-done.20
  166.4 3.6 collective-permute-start.11
  170.0 1.7 collective-permute-start.10
  173.6 1.1 collective-permute-done.9
  176.0 3.6 collective-permute-start.30
  180.8 2.2 fusion.37
  183.0 1.6 collective-permute-done.31
  184.6 1.5 fusion.36
  186.2 3.0 collective-permute-start.39
  189.1 1.5 fusion.35
  190.7 1.3 collective-permute-start.38
  192.0 1.5 fusion.34
  193.6 2.7 fusion.5
  196.3 2.8 fusion.8
  199.1 1.0 collective-permute-start.26
  200.2 1.5 fusion.11
  201.7 2.9 fusion.33
  204.6 3.0 fusion.32
  207.6 120.0 %collective-permute-done.26 = f32[512]{0:T(512)S(1)} collective-permute-done((f32[512]{0:T(512)S(1)}, f32[512]{0:T(512)S(1)}, u32[]{:S(2)}, u32[]{:S(2)}) %collective-permute-start.26) | collective-permute-done | bytes 2080 | tf_op jit(solution)/shard_map/ppermute | solution.py:15
  327.7 2.8 fusion.31
  330.5 2.2 collective-permute-start.36
  332.7 2.8 fusion.30
  335.5 3.2 collective-permute-start.35
  338.6 2.9 fusion.29
  341.6 2.4 collective-permute-start.34
  344.1 2.8 fusion.14
  346.9 1.5 fusion.17
  348.4 4.0 fusion.20
  352.4 2.9 fusion.23
  355.3 5.8 %add_add_fusion.1 = f32[512,1024]{1,0:T(8,128)} fusion(f32[512,1024]{1,0:T(8,128)S(1)} %fusion.5, f32[512,1024]{1,0:T(8,128)S(1)} %fusion.8, f32[512,1024]{1,0:T(8,128)S(1)} %fusion.11, f32[512,1024]{1,0:T(8,128)S(1)} %fusion.14, f32[512,1024]{1,0:T(8,128)S(1)} %fusion.17, f32[512,1024]{1,0:T(8,128)} %fusion.20, f32[512,1024]{1,0:T(8,128)S(1)} %fusion.37, ...), kind=kOutput, calls=%fused_computation.1 | convolution fusion | flops 542638080 | bytes 20975616 | tf_op jit(solution)/shard_map/dot_general | solution.py:121
  361.1 51.8 %collective-permute-done.35 = f32[512,1024]{1,0:T(8,128)S(1)} collective-permute-done((f32[512,1024]{1,0:T(8,128)}, f32[512,1024]{1,0:T(8,128)S(1)}, u32[]{:S(2)}, u32[]{:S(2)}) %collective-permute-start.35) | collective-permute-done | bytes 2097184 | tf_op jit(solution)/shard_map/ppermute | solution.py:15
  413.0 81.8 %collective-permute-done.34 = f32[512,1024]{1,0:T(8,128)S(1)} collective-permute-done((f32[512,1024]{1,0:T(8,128)}, f32[512,1024]{1,0:T(8,128)S(1)}, u32[]{:S(2)}, u32[]{:S(2)}) %collective-permute-start.34) | collective-permute-done | bytes 2097184 | tf_op jit(solution)/shard_map/ppermute | solution.py:15
  494.8 44.9 %collective-permute-done.33 = f32[512,1024]{1,0:T(8,128)S(1)} collective-permute-done((f32[512,1024]{1,0:T(8,128)}, f32[512,1024]{1,0:T(8,128)S(1)}, u32[]{:S(2)}, u32[]{:S(2)}) %collective-permute-start.33) | collective-permute-done | bytes 2097184 | tf_op jit(solution)/shard_map/ppermute | solution.py:15
  539.7 24.9 %collective-permute-done.32 = f32[512,1024]{1,0:T(8,128)S(1)} collective-permute-done((f32[512,1024]{1,0:T(8,128)}, f32[512,1024]{1,0:T(8,128)S(1)}, u32[]{:S(2)}, u32[]{:S(2)}) %collective-permute-start.32) | collective-permute-done | bytes 2097184 | tf_op jit(solution)/shard_map/ppermute | solution.py:15
  564.6 2.9 add_add_fusion
  (135 shorter events, 19.9 us)
Async XLA Ops:
  0.6 12.3 %copy-start = (bf16[512,1024]{1,0:T(8,128)(2,1)S(1)}, bf16[512,1024]{1,0:T(8,128)(2,1)}, u32[]{:S(2)}) copy-start(bf16[512,1024]{1,0:T(8,128)(2,1)} %param.5) | copy-start | bytes 3145732
  0.6 14.4 %copy-start.17 = (s32[1,512]{1,0:T(1,128)S(1)}, s32[1,512]{1,0:T(1,128)}, u32[]{:S(2)}) copy-start(s32[1,512]{1,0:T(1,128)} %param.7) | copy-start | bytes 6148
  0.7 60.1 %collective-permute-start.7 = (bf16[1,512,1024]{2,1,0:T(8,128)(2,1)}, bf16[1,512,1024]{2,1,0:T(8,128)(2,1)S(1)}, u32[]{:S(2)}, u32[]{:S(2)}) collective-permute-start(bf16[1,512,1024]{2,1,0:T(8,128)(2,1)} %bitcast.188), channel_id=1, source_target_pairs={{0,28},{1,29},{2,30},{3,31},{4,0},{5,1},{6,2},{7,3},{8,4},{9,5},{1... | collective-permute-start | bytes 3145736 | tf_op jit(solution)/shard_map/ppermute | solution.py:15
  6.7 70.8 %collective-permute-start.1 = (bf16[1,512,1024]{2,1,0:T(8,128)(2,1)}, bf16[1,512,1024]{2,1,0:T(8,128)(2,1)}, u32[]{:S(2)}, u32[]{:S(2)}) collective-permute-start(bf16[1,512,1024]{2,1,0:T(8,128)(2,1)} %bitcast.189), channel_id=1, source_target_pairs={{0,3},{1,4},{2,5},{3,6},{4,7},{5,8},{6,9},{7,10},{8,11},{9,12},{10... | collective-permute-start | bytes 3145736 | tf_op jit(solution)/shard_map/ppermute | solution.py:15
  7.4 75.5 %collective-permute-start.6 = (bf16[1,512,1024]{2,1,0:T(8,128)(2,1)}, bf16[1,512,1024]{2,1,0:T(8,128)(2,1)}, u32[]{:S(2)}, u32[]{:S(2)}) collective-permute-start(bf16[1,512,1024]{2,1,0:T(8,128)(2,1)} %bitcast.190), channel_id=1, source_target_pairs={{0,29},{1,30},{2,31},{3,0},{4,1},{5,2},{6,3},{7,4},{8,5},{9,6},{10... | collective-permute-start | bytes 3145736 | tf_op jit(solution)/shard_map/ppermute | solution.py:15
  11.2 73.8 %collective-permute-start.5 = (bf16[1,512,1024]{2,1,0:T(8,128)(2,1)}, bf16[1,512,1024]{2,1,0:T(8,128)(2,1)}, u32[]{:S(2)}, u32[]{:S(2)}) collective-permute-start(bf16[1,512,1024]{2,1,0:T(8,128)(2,1)} %bitcast.191), channel_id=1, source_target_pairs={{0,30},{1,31},{2,0},{3,1},{4,2},{5,3},{6,4},{7,5},{8,6},{9,7},{10,... | collective-permute-start | bytes 3145736 | tf_op jit(solution)/shard_map/ppermute | solution.py:15
  11.5 68.8 %collective-permute-start.3 = (bf16[1,512,1024]{2,1,0:T(8,128)(2,1)}, bf16[1,512,1024]{2,1,0:T(8,128)(2,1)}, u32[]{:S(2)}, u32[]{:S(2)}) collective-permute-start(bf16[1,512,1024]{2,1,0:T(8,128)(2,1)} %bitcast.192), channel_id=1, source_target_pairs={{0,1},{1,2},{2,3},{3,4},{4,5},{5,6},{6,7},{7,8},{8,9},{9,10},{10,1... | collective-permute-start | bytes 3145736 | tf_op jit(solution)/shard_map/ppermute | solution.py:15
  12.9 2.8 copy-start.18
  12.9 48.9 %copy-start.19 = (bf16[512,1024]{1,0:T(8,128)(2,1)S(1)}, bf16[512,1024]{1,0:T(8,128)(2,1)}, u32[]{:S(2)}) copy-start(bf16[512,1024]{1,0:T(8,128)(2,1)} %param.6) | copy-start | bytes 3145732
  61.8 62.1 %collective-permute-start.4 = (bf16[1,512,1024]{2,1,0:T(8,128)(2,1)S(1)}, bf16[1,512,1024]{2,1,0:T(8,128)(2,1)S(1)}, u32[]{:S(2)}, u32[]{:S(2)}) collective-permute-start(bf16[1,512,1024]{2,1,0:T(8,128)(2,1)S(1)} %bitcast.193), channel_id=1, source_target_pairs={{0,31},{1,0},{2,1},{3,2},{4,3},{5,4},{6,5},{7,6},{8,7},{9,8},{10,9... | collective-permute-start | bytes 3145736 | tf_op jit(solution)/shard_map/ppermute | solution.py:15
  77.5 42.5 %collective-permute-start.2 = (bf16[1,512,1024]{2,1,0:T(8,128)(2,1)S(1)}, bf16[1,512,1024]{2,1,0:T(8,128)(2,1)S(1)}, u32[]{:S(2)}, u32[]{:S(2)}) collective-permute-start(bf16[1,512,1024]{2,1,0:T(8,128)(2,1)S(1)} %bitcast.194), channel_id=1, source_target_pairs={{0,2},{1,3},{2,4},{3,5},{4,6},{5,7},{6,8},{7,9},{8,10},{9,11},{10,... | collective-permute-start | bytes 3145736 | tf_op jit(solution)/shard_map/ppermute | solution.py:15
  79.6 2.9 copy-start.3
  80.4 47.3 %collective-permute-start = (bf16[1,512,1024]{2,1,0:T(8,128)(2,1)S(1)}, bf16[1,512,1024]{2,1,0:T(8,128)(2,1)S(1)}, u32[]{:S(2)}, u32[]{:S(2)}) collective-permute-start(bf16[1,512,1024]{2,1,0:T(8,128)(2,1)S(1)} %bitcast.195), channel_id=1, source_target_pairs={{0,4},{1,5},{2,6},{3,7},{4,8},{5,9},{6,10},{7,11},{8,12},{9,13},{1... | collective-permute-start | bytes 3145736 | tf_op jit(solution)/shard_map/ppermute | solution.py:15
  82.5 2.4 copy-start.5
  85.0 36.7 %copy-start.11 = (f32[512,512]{1,0:T(8,128)}, f32[512,512]{1,0:T(8,128)S(1)}, u32[]{:S(2)}) copy-start(f32[512,512]{1,0:T(8,128)S(1)} %get-tuple-element.65) | copy-start | bytes 3145732
  87.4 33.8 %copy-start.13 = (f32[512,512]{1,0:T(8,128)}, f32[512,512]{1,0:T(8,128)S(1)}, u32[]{:S(2)}) copy-start(f32[512,512]{1,0:T(8,128)S(1)} %get-tuple-element.66) | copy-start | bytes 3145732
  120.9 3.9 copy-start.7
  123.9 1.2 copy-start.24
  124.8 3.8 copy-start.15
  127.7 6.2 %copy-start.22 = (bf16[1,512,1024]{2,1,0:T(8,128)(2,1)}, bf16[1,512,1024]{2,1,0:T(8,128)(2,1)S(1)}, u32[]{:S(2)}) copy-start(bf16[1,512,1024]{2,1,0:T(8,128)(2,1)S(1)} %collective-permute-done) | copy-start | bytes 3145732
  128.6 5.0 copy-start.9
  139.1 18.7 %collective-permute-start.15 = (f32[512]{0:T(512)S(1)}, f32[512]{0:T(512)S(1)}, u32[]{:S(2)}, u32[]{:S(2)}) collective-permute-start(f32[512]{0:T(512)S(1)} %broadcast_select_fusion.16), channel_id=1, source_target_pairs={{0,4},{1,5},{2,6},{3,7},{4,8},{5,9},{6,10},{7,11},{8,12},{9,13},{1... | collective-permute-start | bytes 6152 | tf_op jit(solution)/shard_map/ppermute | solution.py:15
  139.2 19.3 %collective-permute-start.14 = (f32[512]{0:T(512)S(1)}, f32[512]{0:T(512)S(1)}, u32[]{:S(2)}, u32[]{:S(2)}) collective-permute-start(f32[512]{0:T(512)S(1)} %broadcast_select_fusion.17), channel_id=1, source_target_pairs={{0,3},{1,4},{2,5},{3,6},{4,7},{5,8},{6,9},{7,10},{8,11},{9,12},{10... | collective-permute-start | bytes 6152 | tf_op jit(solution)/shard_map/ppermute | solution.py:15
  143.1 16.7 %collective-permute-start.13 = (f32[512]{0:T(512)S(1)}, f32[512]{0:T(512)S(1)}, u32[]{:S(2)}, u32[]{:S(2)}) collective-permute-start(f32[512]{0:T(512)S(1)} %broadcast_select_fusion.18), channel_id=1, source_target_pairs={{0,2},{1,3},{2,4},{3,5},{4,6},{5,7},{6,8},{7,9},{8,10},{9,11},{10,... | collective-permute-start | bytes 6152 | tf_op jit(solution)/shard_map/ppermute | solution.py:15
  148.6 11.2 %collective-permute-start.16 = (f32[512]{0:T(512)S(1)}, f32[512]{0:T(512)S(1)}, u32[]{:S(2)}, u32[]{:S(2)}) collective-permute-start(f32[512]{0:T(512)S(1)} %broadcast_select_fusion.7), channel_id=1, source_target_pairs={{0,28},{1,29},{2,30},{3,31},{4,0},{5,1},{6,2},{7,3},{8,4},{9,5},{1... | collective-permute-start | bytes 6152 | tf_op jit(solution)/shard_map/ppermute | solution.py:15
  153.8 7.3 %collective-permute-start.17 = (f32[512]{0:T(512)S(1)}, f32[512]{0:T(512)S(1)}, u32[]{:S(2)}, u32[]{:S(2)}) collective-permute-start(f32[512]{0:T(512)S(1)} %broadcast_select_fusion.6), channel_id=1, source_target_pairs={{0,29},{1,30},{2,31},{3,0},{4,1},{5,2},{6,3},{7,4},{8,5},{9,6},{10... | collective-permute-start | bytes 6152 | tf_op jit(solution)/shard_map/ppermute | solution.py:15
  157.8 5.4 collective-permute-start.18
  158.6 6.0 %collective-permute-start.19 = (f32[512]{0:T(512)S(1)}, f32[512]{0:T(512)S(1)}, u32[]{:S(2)}, u32[]{:S(2)}) collective-permute-start(f32[512]{0:T(512)S(1)} %broadcast_select_fusion.4), channel_id=1, source_target_pairs={{0,31},{1,0},{2,1},{3,2},{4,3},{5,4},{6,5},{7,6},{8,7},{9,8},{10,9... | collective-permute-start | bytes 6152 | tf_op jit(solution)/shard_map/ppermute | solution.py:15
  159.8 6.6 %collective-permute-start.20 = (f32[512]{0:T(512)S(1)}, f32[512]{0:T(512)S(1)}, u32[]{:S(2)}, u32[]{:S(2)}) collective-permute-start(f32[512]{0:T(512)S(1)} %broadcast_select_fusion.3), channel_id=1, source_target_pairs={{0,1},{1,2},{2,3},{3,4},{4,5},{5,6},{6,7},{7,8},{8,9},{9,10},{10,1... | collective-permute-start | bytes 6152 | tf_op jit(solution)/shard_map/ppermute | solution.py:15
  159.8 10.2 %collective-permute-start.21 = (f32[512]{0:T(512)S(1)}, f32[512]{0:T(512)S(1)}, u32[]{:S(2)}, u32[]{:S(2)}) collective-permute-start(f32[512]{0:T(512)S(1)} %broadcast_select_fusion.2), channel_id=1, source_target_pairs={{0,2},{1,3},{2,4},{3,5},{4,6},{5,7},{6,8},{7,9},{8,10},{9,11},{10,... | collective-permute-start | bytes 6152 | tf_op jit(solution)/shard_map/ppermute | solution.py:15
  161.1 10.6 %collective-permute-start.22 = (f32[512]{0:T(512)S(1)}, f32[512]{0:T(512)S(1)}, u32[]{:S(2)}, u32[]{:S(2)}) collective-permute-start(f32[512]{0:T(512)S(1)} %broadcast_select_fusion.1), channel_id=1, source_target_pairs={{0,3},{1,4},{2,5},{3,6},{4,7},{5,8},{6,9},{7,10},{8,11},{9,12},{10... | collective-permute-start | bytes 6152 | tf_op jit(solution)/shard_map/ppermute | solution.py:15
  163.2 8.4 %collective-permute-start.23 = (f32[512]{0:T(512)S(1)}, f32[512]{0:T(512)S(1)}, u32[]{:S(2)}, u32[]{:S(2)}) collective-permute-start(f32[512]{0:T(512)S(1)} %get-tuple-element.72), channel_id=1, source_target_pairs={{0,4},{1,5},{2,6},{3,7},{4,8},{5,9},{6,10},{7,11},{8,12},{9,13},{1... | collective-permute-start | bytes 6152 | tf_op jit(solution)/shard_map/ppermute | solution.py:15
  164.6 8.4 %collective-permute-start.12 = (f32[512]{0:T(512)S(1)}, f32[512]{0:T(512)S(1)}, u32[]{:S(2)}, u32[]{:S(2)}) collective-permute-start(f32[512]{0:T(512)S(1)} %broadcast_select_fusion.19), channel_id=1, source_target_pairs={{0,1},{1,2},{2,3},{3,4},{4,5},{5,6},{6,7},{7,8},{8,9},{9,10},{10,1... | collective-permute-start | bytes 6152 | tf_op jit(solution)/shard_map/ppermute | solution.py:15
  166.4 6.7 %collective-permute-start.11 = (f32[512]{0:T(512)S(1)}, f32[512]{0:T(512)S(1)}, u32[]{:S(2)}, u32[]{:S(2)}) collective-permute-start(f32[512]{0:T(512)S(1)} %broadcast_select_fusion.20), channel_id=1, source_target_pairs={{0,31},{1,0},{2,1},{3,2},{4,3},{5,4},{6,5},{7,6},{8,7},{9,8},{10,9... | collective-permute-start | bytes 6152 | tf_op jit(solution)/shard_map/ppermute | solution.py:15
  170.0 3.6 collective-permute-start.10
  171.7 3.0 collective-permute-start.9
  171.7 3.6 collective-permute-start.8
  176.0 13.1 %collective-permute-start.30 = (f32[512]{0:T(512)S(1)}, f32[512]{0:T(512)S(1)}, u32[]{:S(2)}, u32[]{:S(2)}) collective-permute-start(f32[512]{0:T(512)S(1)} %get-tuple-element.51), channel_id=1, source_target_pairs={{0,29},{1,30},{2,31},{3,0},{4,1},{5,2},{6,3},{7,4},{8,5},{9,6},{10... | collective-permute-start | bytes 6152 | tf_op jit(solution)/shard_map/ppermute | solution.py:15
  179.6 12.4 %collective-permute-start.29 = (f32[512]{0:T(512)S(1)}, f32[512]{0:T(512)S(1)}, u32[]{:S(2)}, u32[]{:S(2)}) collective-permute-start(f32[512]{0:T(512)S(1)} %get-tuple-element.51), channel_id=1, source_target_pairs={{0,30},{1,31},{2,0},{3,1},{4,2},{5,3},{6,4},{7,5},{8,6},{9,7},{10,... | collective-permute-start | bytes 6152 | tf_op jit(solution)/shard_map/ppermute | solution.py:15
  180.1 19.0 %collective-permute-start.28 = (f32[512]{0:T(512)S(1)}, f32[512]{0:T(512)S(1)}, u32[]{:S(2)}, u32[]{:S(2)}) collective-permute-start(f32[512]{0:T(512)S(1)} %get-tuple-element.51), channel_id=1, source_target_pairs={{0,31},{1,0},{2,1},{3,2},{4,3},{5,4},{6,5},{7,6},{8,7},{9,8},{10,9... | collective-permute-start | bytes 6152 | tf_op jit(solution)/shard_map/ppermute | solution.py:15
  180.8 23.9 %collective-permute-start.27 = (f32[512]{0:T(512)S(1)}, f32[512]{0:T(512)S(1)}, u32[]{:S(2)}, u32[]{:S(2)}) collective-permute-start(f32[512]{0:T(512)S(1)} %get-tuple-element.51), channel_id=1, source_target_pairs={{0,1},{1,2},{2,3},{3,4},{4,5},{5,6},{6,7},{7,8},{8,9},{9,10},{10,1... | collective-permute-start | bytes 6152 | tf_op jit(solution)/shard_map/ppermute | solution.py:15
  180.8 3.8 collective-permute-start.31
  183.0 6.2 %copy-start.12 = (f32[512,512]{1,0:T(8,128)S(1)}, f32[512,512]{1,0:T(8,128)}, u32[]{:S(2)}) copy-start(f32[512,512]{1,0:T(8,128)} %copy-done.11) | copy-start | bytes 3145732
  186.1 5.8 %copy-start.14 = (f32[512,512]{1,0:T(8,128)S(1)}, f32[512,512]{1,0:T(8,128)}, u32[]{:S(2)}) copy-start(f32[512,512]{1,0:T(8,128)} %copy-done.13) | copy-start | bytes 3145732
  186.2 155.4 %collective-permute-start.39 = (f32[512,1024]{1,0:T(8,128)S(1)}, f32[512,1024]{1,0:T(8,128)S(1)}, u32[]{:S(2)}, u32[]{:S(2)}) collective-permute-start(f32[512,1024]{1,0:T(8,128)S(1)} %fusion.36), channel_id=1, source_target_pairs={{0,4},{1,5},{2,6},{3,7},{4,8},{5,9},{6,10},{7,11},{8,12},{9,13},{1... | collective-permute-start | bytes 6291464 | tf_op jit(solution)/shard_map/ppermute | solution.py:15
  190.7 153.3 %collective-permute-start.38 = (f32[512,1024]{1,0:T(8,128)S(1)}, f32[512,1024]{1,0:T(8,128)S(1)}, u32[]{:S(2)}, u32[]{:S(2)}) collective-permute-start(f32[512,1024]{1,0:T(8,128)S(1)} %fusion.35), channel_id=1, source_target_pairs={{0,3},{1,4},{2,5},{3,6},{4,7},{5,8},{6,9},{7,10},{8,11},{9,12},{10... | collective-permute-start | bytes 6291464 | tf_op jit(solution)/shard_map/ppermute | solution.py:15
  193.5 150.5 %collective-permute-start.37 = (f32[512,1024]{1,0:T(8,128)S(1)}, f32[512,1024]{1,0:T(8,128)S(1)}, u32[]{:S(2)}, u32[]{:S(2)}) collective-permute-start(f32[512,1024]{1,0:T(8,128)S(1)} %fusion.34), channel_id=1, source_target_pairs={{0,2},{1,3},{2,4},{3,5},{4,6},{5,7},{6,8},{7,9},{8,10},{9,11},{10,... | collective-permute-start | bytes 6291464 | tf_op jit(solution)/shard_map/ppermute | solution.py:15
  196.3 3.9 copy-start.16
  196.3 3.9 copy-start.25
  199.1 128.5 %collective-permute-start.26 = (f32[512]{0:T(512)S(1)}, f32[512]{0:T(512)S(1)}, u32[]{:S(2)}, u32[]{:S(2)}) collective-permute-start(f32[512]{0:T(512)S(1)} %get-tuple-element.51), channel_id=1, source_target_pairs={{0,2},{1,3},{2,4},{3,5},{4,6},{5,7},{6,8},{7,9},{8,10},{9,11},{10,... | collective-permute-start | bytes 6152 | tf_op jit(solution)/shard_map/ppermute | solution.py:15
  201.7 3.0 copy-start.6
  204.6 123.0 %copy-start.8 = (f32[512,512]{1,0:T(8,128)S(1)}, f32[512,512]{1,0:T(8,128)}, u32[]{:S(2)}) copy-start(f32[512,512]{1,0:T(8,128)} %copy-done.7) | copy-start | bytes 3145732
  204.6 125.9 %collective-permute-start.25 = (f32[512]{0:T(512)S(1)}, f32[512]{0:T(512)S(1)}, u32[]{:S(2)}, u32[]{:S(2)}) collective-permute-start(f32[512]{0:T(512)S(1)} %get-tuple-element.51), channel_id=1, source_target_pairs={{0,3},{1,4},{2,5},{3,6},{4,7},{5,8},{6,9},{7,10},{8,11},{9,12},{10... | collective-permute-start | bytes 6152 | tf_op jit(solution)/shard_map/ppermute | solution.py:15
  207.6 125.1 %copy-start.4 = (f32[512,512]{1,0:T(8,128)S(1)}, f32[512,512]{1,0:T(8,128)}, u32[]{:S(2)}) copy-start(f32[512,512]{1,0:T(8,128)} %copy-done.3) | copy-start | bytes 3145732
  327.6 7.8 %collective-permute-start.24 = (f32[512]{0:T(512)S(1)}, f32[512]{0:T(512)S(1)}, u32[]{:S(2)}, u32[]{:S(2)}) collective-permute-start(f32[512]{0:T(512)S(1)} %get-tuple-element.51), channel_id=1, source_target_pairs={{0,4},{1,5},{2,6},{3,7},{4,8},{5,9},{6,10},{7,11},{8,12},{9,13},{1... | collective-permute-start | bytes 6152 | tf_op jit(solution)/shard_map/ppermute | solution.py:15
  330.5 8.2 %copy-start.10 = (f32[512,512]{1,0:T(8,128)S(1)}, f32[512,512]{1,0:T(8,128)}, u32[]{:S(2)}) copy-start(f32[512,512]{1,0:T(8,128)} %copy-done.9) | copy-start | bytes 3145732
  330.5 30.6 %collective-permute-start.36 = (f32[512,1024]{1,0:T(8,128)}, f32[512,1024]{1,0:T(8,128)S(1)}, u32[]{:S(2)}, u32[]{:S(2)}) collective-permute-start(f32[512,1024]{1,0:T(8,128)} %fusion.33), channel_id=1, source_target_pairs={{0,1},{1,2},{2,3},{3,4},{4,5},{5,6},{6,7},{7,8},{8,9},{9,10},{10,1... | collective-permute-start | bytes 6291464 | tf_op jit(solution)/shard_map/ppermute | solution.py:15
  335.5 77.5 %collective-permute-start.35 = (f32[512,1024]{1,0:T(8,128)}, f32[512,1024]{1,0:T(8,128)S(1)}, u32[]{:S(2)}, u32[]{:S(2)}) collective-permute-start(f32[512,1024]{1,0:T(8,128)} %fusion.32), channel_id=1, source_target_pairs={{0,31},{1,0},{2,1},{3,2},{4,3},{5,4},{6,5},{7,6},{8,7},{9,8},{10,9... | collective-permute-start | bytes 6291464 | tf_op jit(solution)/shard_map/ppermute | solution.py:15
  341.6 5.3 copy-start.21
  341.6 153.2 %collective-permute-start.34 = (f32[512,1024]{1,0:T(8,128)}, f32[512,1024]{1,0:T(8,128)S(1)}, u32[]{:S(2)}, u32[]{:S(2)}) collective-permute-start(f32[512,1024]{1,0:T(8,128)} %fusion.31), channel_id=1, source_target_pairs={{0,30},{1,31},{2,0},{3,1},{4,2},{5,3},{6,4},{7,5},{8,6},{9,7},{10,... | collective-permute-start | bytes 6291464 | tf_op jit(solution)/shard_map/ppermute | solution.py:15
  344.0 195.7 %collective-permute-start.33 = (f32[512,1024]{1,0:T(8,128)}, f32[512,1024]{1,0:T(8,128)S(1)}, u32[]{:S(2)}, u32[]{:S(2)}) collective-permute-start(f32[512,1024]{1,0:T(8,128)} %fusion.30), channel_id=1, source_target_pairs={{0,29},{1,30},{2,31},{3,0},{4,1},{5,2},{6,3},{7,4},{8,5},{9,6},{10... | collective-permute-start | bytes 6291464 | tf_op jit(solution)/shard_map/ppermute | solution.py:15
  344.0 220.6 %collective-permute-start.32 = (f32[512,1024]{1,0:T(8,128)}, f32[512,1024]{1,0:T(8,128)S(1)}, u32[]{:S(2)}, u32[]{:S(2)}) collective-permute-start(f32[512,1024]{1,0:T(8,128)} %fusion.29), channel_id=1, source_target_pairs={{0,28},{1,29},{2,30},{3,31},{4,0},{5,1},{6,2},{7,3},{8,4},{9,5},{1... | collective-permute-start | bytes 6291464 | tf_op jit(solution)/shard_map/ppermute | solution.py:15
  348.4 4.1 copy-start.23
  352.4 2.9 copy-start.2
  (2 other events, 2.3 us)
where the time goes:
time: 568 us; the launch traced here: 567 us
  waiting for transfers between devices  406 us (71%)
  starting transfers between devices  69.7 us (12%)
  matrix products  63.3 us (11%)
  other arithmetic  25.1 us (4%)
    ppermute x40, waiting for transfers between devices, shifted(): lax.ppermute(value, axis, [(i, (i + by) % peers) for i in range(peers)])  406 us
    ppermute x40, starting transfers between devices, shifted(): lax.ppermute(value, axis, [(i, (i + by) % peers) for i in range(peers)])  69.7 us
    dot_general x9, matrix products, make_terms(): jnp.dot(weight, passage_rows, preferred_element_type=jnp.float32)  26.2 us
    dot_general x9, matrix products, transposed_product(): lax.dot_general(weight, rows, (((0,), (0,)), ((), ())), preferred_element...  21.9 us
    dot_general x9, matrix products, scores_of(): lax.dot_general(query_rows, passage_rows, (((1,), (1,)), ((), ())), prefe...  15.3 us
  transfers between devices with their start and end apart: 40, of which 12 were waited for; matrix products, arithmetic and copies ran while one was open for 13% of the time, Pallas kernels for 0%

commit v1 on v0

v1 whole, which is shorter than its diff:
```python
import functools

import jax
import jax.numpy as jnp
from jax import lax
from jax.experimental import pallas as pl
from jax.experimental.pallas import tpu as pltpu
from jax.sharding import PartitionSpec as P

RANGE = 4
OWN = RANGE
SLOTS = 2 * RANGE + 1
MESH = pl.DeviceIdType.MESH
SCALE = 20.0
FAR = -1.0e30

NT = (((1,), (1,)), ((), ()))


def kernel(chips, q_hbm, p_hbm, bias_ref, pos_col, pos_row, gq_ref, gp_ref, loss_ref,
           buf, relay, sc, tops, totals, bbuf, lbuf,
           load_sem, send_sem, recv_sem, relay_sem, bsend, brecv, lsend, lrecv):
    chip = lax.axis_index("dp")
    core = lax.axis_index("cores")
    me = 2 * chip + core
    blocks = 2 * chips
    j = chip % 4
    sigma = 1 - 2 * (j // 2)
    is_a = 1 - ((j + 1) // 2) % 2
    tau = sigma * (2 * is_a - 1)
    which = j // 2

    def device(block):
        block = (block + blocks) % blocks
        return (block // 2, block % 2)

    sibling = (chip, 1 - core)
    x_dev = ((chip + tau + chips) % chips, core)
    y_dev = ((chip + 2 * sigma + chips) % chips, core)
    z_dev = ((chip + 4 * sigma + chips) % chips, core)

    def at(k):
        return OWN + 2 * k

    xs, ys, zs, fs = at(tau), at(2 * sigma), at(-2 * sigma), at(-tau)
    turn = 1 - 2 * core

    loads = [
        pltpu.make_async_copy(q_hbm, buf.at[OWN, 0], load_sem.at[0]),
        pltpu.make_async_copy(p_hbm, buf.at[OWN, 1], load_sem.at[1]),
    ]
    for load in loads:
        load.start()

    barrier = pltpu.get_barrier_semaphore()
    others = [o for o in range(-RANGE, RANGE + 1) if o != 0]
    greeted = others + [-8, 8]
    for o in greeted:
        pl.semaphore_signal(barrier, inc=1, device_id=device(me + o), device_id_type=MESH)
    bbuf[OWN] = bias_ref[...]
    for load in loads:
        load.wait()
    pl.semaphore_wait(barrier, len(greeted))

    def put(src, dst, to, sent, got):
        return pltpu.make_async_remote_copy(
            src_ref=src, dst_ref=dst, send_sem=sent, recv_sem=got, device_id=to, device_id_type=MESH
        )

    def block(slot, m, to, to_slot, n):
        return put(buf.at[slot, m], buf.at[to_slot, m], to, send_sem.at[n], recv_sem.at[to_slot, m])

    def bias_copy(o):
        slot = OWN - o
        return put(bbuf.at[OWN], bbuf.at[slot], device(me + o), bsend.at[OWN + o], brecv.at[slot])

    def lse_copy(o):
        slot = OWN - o
        return put(lbuf.at[OWN], lbuf.at[slot], device(me + o), lsend.at[OWN + o], lrecv.at[slot])

    own_x = [block(OWN, m, x_dev, at(-tau), m) for m in range(2)]
    own_y = [block(OWN, m, y_dev, at(-2 * sigma), 2 + m) for m in range(2)]
    own_s = [block(OWN, m, sibling, OWN - turn, 4 + m) for m in range(2)]
    for m in range(2):
        own_x[m].start()
        own_y[m].start()
        if m == 0:
            for o in others:
                bias_copy(o).start()
    for m in range(2):
        own_s[m].start()

    def forward(slot, m, n):
        return block(slot, m, sibling, slot - turn, n)

    def forwarded(slot):
        return jnp.logical_and(slot - turn >= 0, slot - turn < SLOTS)

    diag_y = [block(xs, m, y_dev, at(-sigma), 6) for m in range(2)]
    diag_x = [block(ys, m, x_dev, at(sigma), 7) for m in range(2)]
    to_z = [block(ys, m, z_dev, at(-2 * sigma), 8 + m) for m in range(2)]
    to_relay = put(buf.at[xs, 1], relay, y_dev, send_sem.at[10], relay_sem.at[0])
    from_relay = put(relay, buf.at[at(-sigma), 1], z_dev, send_sem.at[10], recv_sem.at[at(-sigma), 1])
    last_x = block(zs, 0, x_dev, at(-sigma), 11)

    tops[...] = jnp.full(tops.shape, FAR, jnp.float32)
    totals[...] = jnp.zeros(totals.shape, jnp.float32)

    sib = [s + turn for s in (OWN, xs, ys, zs, fs)]
    plan = [
        (OWN, 0), (OWN, 1), (sib[0], 0), (sib[0], 1),
        (xs, 0), (ys, 0), (xs, 1), (ys, 1),
        (sib[1], 0), (sib[2], 0), (sib[1], 1), (sib[2], 1),
        (zs, 0), (zs, 1), (fs, 0), (fs, 1),
        (sib[3], 0), (sib[3], 1), (sib[4], 0), (sib[4], 1),
    ]

    def event(e, carry):
        slot = jnp.int32(OWN)
        m = jnp.int32(0)
        for i, (s, which_m) in enumerate(plan):
            slot = jnp.where(e == i, s, slot)
            m = jnp.where(e == i, which_m, m)
        present = jnp.logical_and(slot >= 0, slot < SLOTS)
        slot = jnp.where(present, slot, 0)
        side = 1 - m

        @pl.when(jnp.logical_and(e == 8, is_a == 1))
        def _():
            put(relay, relay, sibling, send_sem.at[10], relay_sem.at[0]).wait_recv()
            from_relay.start()

        @pl.when(jnp.logical_and(e > 1, present))
        def _():
            block(slot, m, sibling, slot, 0).wait_recv()

            @pl.when(m == 0)
            def _():
                put(bbuf.at[slot], bbuf.at[slot], sibling, bsend.at[0], brecv.at[slot]).wait_recv()

        for i in (5, 7):
            @pl.when(e == i)
            def _():
                to_z[i // 6].start()

                @pl.when(jnp.logical_and(is_a == 1, which == i // 6))
                def _():
                    diag_x[i // 6].start()

        for i in (4, 6):
            @pl.when(jnp.logical_and(jnp.logical_and(e == i, is_a == 1), which == i // 6))
            def _():
                diag_y[i // 6].start()

        @pl.when(jnp.logical_and(e == 6, is_a == 0))
        def _():
            to_relay.start()

        @pl.when(jnp.logical_and(e == 12, is_a == 0))
        def _():
            last_x.start()

        for i in (4, 5, 6, 7, 12, 13, 14, 15):
            s, which_m = plan[i]

            @pl.when(jnp.logical_and(e == i, forwarded(s)))
            def _():
                forward(s, which_m, 8 + i if i >= 12 else 12 + i - 4).start()

        @pl.when(present)
        def _():
            bias = bbuf[jnp.where(side == 0, OWN, slot), pl.ds(jnp.where(side == 0, slot, SLOTS - 1 - slot), 1), :]
            rows = buf.shape[2]
            for r in range(0, rows, rows // 2):
                part = pl.ds(r, rows // 2)
                s = SCALE * lax.dot_general(
                    buf[OWN, side, part, :], buf[slot, m], NT, preferred_element_type=jnp.float32
                ) + bias
                sc[slot, side, part, :] = s
                old = tops[side, part, :]
                top = jnp.maximum(old, jnp.max(s, axis=1, keepdims=True))
                total = totals[side, part, :] * jnp.exp(old - top)
                totals[side, part, :] = total + jnp.sum(jnp.exp(s - top), axis=1, keepdims=True)
                tops[side, part, :] = top

        return carry

    lax.fori_loop(0, len(plan), event, 0)

    rows = buf.shape[2]
    for side in range(2):
        lse = tops[side] + jnp.log(totals[side])
        tops[side] = lse
        lbuf[OWN, side] = jnp.transpose(jnp.broadcast_to(lse, (rows, 128)))[0:8]
    for o in others:
        lse_copy(o).start()

    grads = (gq_ref, gp_ref)

    def gradient(slot, side, own):
        other = lbuf[slot, 1 - side, 0:1, :]
        for r in range(0, rows, rows // 2):
            part = pl.ds(r, rows // 2)
            s = sc[slot, side, part, :]
            w = jnp.exp(s - tops[side, part, :]) + jnp.exp(s - other)
            if own:
                if side == 0:
                    hit = pos_col[part, :] == lax.broadcasted_iota(jnp.int32, s.shape, 1)
                else:
                    hit = pos_row[...] == lax.broadcasted_iota(jnp.int32, s.shape, 0) + r
                e = hit.astype(jnp.float32)
                w = w - 2.0 * e
                totals[side, part, :] = tops[side, part, :] - jnp.sum(s * e, axis=1, keepdims=True)
            w = (SCALE * w).astype(jnp.bfloat16)
            term = jnp.dot(w, buf[slot, 1 - side], preferred_element_type=jnp.float32)
            if own:
                grads[side][part, :] = term
            else:
                grads[side][part, :] += term

    for side in range(2):
        gradient(OWN, side, True)
        loss_ref[side] = jnp.transpose(jnp.broadcast_to(totals[side], (rows, 128)))[0:8]

    def later(t, carry):
        slot = t + t // RANGE
        put(lbuf.at[slot], lbuf.at[slot], sibling, lsend.at[0], lrecv.at[slot]).wait_recv()
        for side in range(2):
            gradient(slot, side, False)
        return carry

    lax.fori_loop(0, SLOTS - 1, later, 0)

    for copy in own_x + own_y + own_s + to_z:
        copy.wait_send()
    for i in (4, 5, 6, 7, 12, 13, 14, 15):
        s, which_m = plan[i]

        @pl.when(forwarded(s))
        def _():
            forward(s, which_m, 8 + i if i >= 12 else 12 + i - 4).wait_send()

    @pl.when(is_a == 1)
    def _():
        diag_y[0].wait_send()
        diag_x[0].wait_send()
        from_relay.wait_send()

    @pl.when(is_a == 0)
    def _():
        to_relay.wait_send()
        last_x.wait_send()

    for o in others:
        bias_copy(o).wait_send()
        lse_copy(o).wait_send()


def present_pairs(pair_blocks, negative_pair_count, block, blocks):
    listed = pair_blocks.shape[1]
    used = jnp.arange(listed, dtype=jnp.int32) < negative_pair_count[0]
    offsets = jnp.arange(-RANGE, RANGE + 1, dtype=jnp.int32)
    target = (block + offsets) % blocks
    found = jnp.any((pair_blocks[0][None, :] == target[:, None]) & used[None, :], axis=1)
    return found | (offsets == 0)


def solution(mesh):
    chips = mesh.shape["dp"]
    blocks = chips * mesh.shape["cores"]

    def body(queries, passages, positives, pair_blocks, negative_pair_count):
        rows, width = queries.shape
        block = lax.axis_index(("dp", "cores"))
        present = present_pairs(pair_blocks, negative_pair_count, block, blocks)
        bias = jnp.where(present, 0.0, FAR).astype(jnp.float32)
        bias = jnp.broadcast_to(jnp.pad(bias, (0, 16 - SLOTS))[:, None], (16, rows))
        vmem = pl.BlockSpec(memory_space=pltpu.VMEM)
        anywhere = pl.BlockSpec(memory_space=pl.ANY)
        gq, gp, loss = pl.pallas_call(
            functools.partial(kernel, chips),
            out_shape=(
                jax.ShapeDtypeStruct((rows, width), jnp.float32),
                jax.ShapeDtypeStruct((rows, width), jnp.float32),
                jax.ShapeDtypeStruct((2, 8, rows), jnp.float32),
            ),
            in_specs=[anywhere, anywhere, vmem, vmem, vmem],
            out_specs=(vmem, vmem, vmem),
            scratch_shapes=[
                pltpu.VMEM((SLOTS, 2, rows, width), jnp.bfloat16),
                pltpu.VMEM((rows, width), jnp.bfloat16),
                pltpu.VMEM((SLOTS, 2, rows, rows), jnp.float32),
                pltpu.VMEM((2, rows, 1), jnp.float32),
                pltpu.VMEM((2, rows, 1), jnp.float32),
                pltpu.VMEM((SLOTS, 16, rows), jnp.float32),
                pltpu.VMEM((SLOTS, 2, 8, rows), jnp.float32),
                pltpu.SemaphoreType.DMA((2,)),
                pltpu.SemaphoreType.DMA((24,)),
                pltpu.SemaphoreType.DMA((SLOTS, 2)),
                pltpu.SemaphoreType.DMA((1,)),
                pltpu.SemaphoreType.DMA((SLOTS,)),
                pltpu.SemaphoreType.DMA((SLOTS,)),
                pltpu.SemaphoreType.DMA((SLOTS,)),
                pltpu.SemaphoreType.DMA((SLOTS,)),
            ],
            compiler_params=pltpu.CompilerParams(
                collective_id=0, has_side_effects=True, vmem_limit_bytes=58 * 2**20
            ),
            cost_estimate=pl.CostEstimate(
                flops=36 * 2 * rows * rows * width,
                bytes_accessed=12 * rows * width,
                transcendentals=54 * rows * rows,
            ),
        )(queries, passages, bias, positives.reshape(rows, 1), positives)
        return loss[0, 0:1], loss[1, 0:1], gq, gp

    split = P(("dp", "cores"), None)
    return jax.shard_map(
        body,
        mesh=mesh,
        in_specs=(split, split, split, split, P(("dp", "cores"))),
        out_specs=(split, split, split, split),
        check_vma=False,
    )
```

time: 568 us -> 140 us (0.25)
  waiting for transfers between devices: 406 us -> 0 us
  Pallas kernels: 0 us -> 128 us
  starting transfers between devices: 69.7 us -> 0 us
  matrix products: 63.3 us -> 0 us
  other arithmetic: 25.1 us -> 0.78 us
  local copies, waits for them, and re-layouts: 1.37 us -> 8.18 us
    ppermute x40 -> x0, waiting for transfers between devices: 406 us -> none  [shifted(): lax.ppermute(value, axis, [(i, (i + by) % peers) for i in range(peers)])]
    pallas_call x0 -> x1, Pallas kernels: none -> 128 us  [body(): pl.pallas_call(functools.partial(kernel, chips), out_shape=(jax.ShapeDtyp...]
    ppermute x40 -> x0, starting transfers between devices: 69.7 us -> none  [shifted(): lax.ppermute(value, axis, [(i, (i + by) % peers) for i in range(peers)])]
    dot_general x27 -> x0, matrix products: 63.3 us -> none  [the longest x9 26.2 us: make_terms(): jnp.dot(weight, passage_rows, preferred_element_type=jnp.float32)]
    select_n x19 -> x2, other arithmetic: 14.4 us -> 0.02 us  [the longest x1 0.02 us: present_pairs(): target = (block + offsets) % blocks]
  transfers between devices with their start and end apart: 40 -> 0, of which waited for: 12 -> 0; matrix products, arithmetic and copies ran while one was open for 13% -> 0% of each run, Pallas kernels for 0% -> 0%
where the time goes in v1:
time: 140 us; the launch traced here: 138 us
  Pallas kernels  128 us (91%)
  local copies, waits for them, and re-layouts  8.18 us (6%)
    pallas_call x1, Pallas kernels, body(): pl.pallas_call(functools.partial(kernel, chips), out_shape=(jax.ShapeDtyp...  128 us
    unnamed x4, local copies, waits for them, and re-layouts  4.63 us

profile of v1, /device:TPU:0, one launch (start us, length us, event | category | flops | bytes accessed | tf_op | source)
XLA Modules:
  0.0 138.4 jit_solution(4063565067606035749)
XLA Ops:
  1.3 0.7 and_reduce_fusion
  2.1 0.7 broadcast_in_dim.18.bias_ref
  2.8 1.5 %copy.10.pos_col = s32[512,1]{1,0:T(8,128)} copy(s32[512,1]{0,1:T(1,128)} %bitcast.8) | data formatting | bytes 4096 | tf_op jit(solution)/shard_map/reshape | solution.py:314
  4.3 128.2 %shard_map.84 = (f32[512,1024]{1,0:T(8,128)}, f32[512,1024]{1,0:T(8,128)}, f32[2,8,512]{2,1,0:T(8,128)}) custom-call(bf16[512,1024]{1,0:T(8,128)(2,1)} %q_hbm.1, bf16[512,1024]{1,0:T(8,128)(2,1)} %p_hbm.1, f32[16,512]{1,0:T(8,128)} %broadcast_in_dim.18.bias_ref, s32[512,1]{1,0:T(8,128)} %copy.10.pos_col, s32[1,512]{1,0:T(1,128)} %pos_row.1), custom_call_target="tpu_custom_call" | custom-call | flops 19327352832 | bytes 6291456 | tf_op jit(solution)/shard_map/pallas_call | solution.py:280
  132.5 1.3 slice_bitcast_fusion
  133.8 0.0 copy-start
  133.8 3.3 %copy.14 = f32[512,1024]{1,0:T(8,128)} copy(f32[512,1024]{1,0:T(8,128)} %get-tuple-element.18) | data formatting | bytes 4194304
  137.1 0.0 copy-done
  137.1 1.3 copy.15
  (4 shorter events, 0.0 us)
Async XLA Ops:
  133.8 3.3 %copy-start = (f32[512,1024]{1,0:T(8,128)S(1)}, f32[512,1024]{1,0:T(8,128)}, u32[]{:S(2)}) copy-start(f32[512,1024]{1,0:T(8,128)} %get-tuple-element.19) | copy-start | bytes 6291460

commit v2 on v1

v2 whole, which is shorter than its diff:
```python
import functools

import jax
import jax.numpy as jnp
from jax import lax
from jax.experimental import pallas as pl
from jax.experimental.pallas import tpu as pltpu
from jax.sharding import PartitionSpec as P

RANGE = 4
OWN = RANGE
SLOTS = 2 * RANGE + 1
PASSING = SLOTS
MESH = pl.DeviceIdType.MESH
SCALE = 20.0
FAR = -1.0e30

NT = (((1,), (1,)), ((), ()))


def kernel(chips, q_hbm, p_hbm, bias_ref, pos_col, pos_row, gq_ref, gp_ref, loss_ref,
           buf, sc, tops, totals, bbuf, lbuf,
           load_sem, send_sem, recv_sem, bsend, brecv, lsend, lrecv):
    chip = lax.axis_index("dp")
    core = lax.axis_index("cores")
    me = 2 * chip + core
    blocks = 2 * chips
    j = chip % 4
    sigma = 1 - 2 * (j // 2)
    corner = ((j + 1) // 2) % 2 == 0
    tau = jnp.where(corner, sigma, -sigma)
    across = j // 2

    def device(block):
        block = (block + blocks) % blocks
        return (block // 2, block % 2)

    sibling = (chip, 1 - core)
    x_dev = ((chip + tau + chips) % chips, core)
    y_dev = ((chip + 2 * sigma + chips) % chips, core)
    z_dev = ((chip + 4 * sigma + chips) % chips, core)

    def at(k):
        return OWN + 2 * k

    xs, ys, zs, fs = at(tau), at(2 * sigma), at(-2 * sigma), at(-tau)
    turn = 1 - 2 * core
    half = buf.shape[3]
    rows = 2 * half

    loads = []
    for m, ref in enumerate((q_hbm, p_hbm)):
        for h in range(2):
            loads.append(pltpu.make_async_copy(
                ref.at[pl.ds(h * half, half)], buf.at[OWN, m, h], load_sem.at[2 * m + h]))
    for load in loads:
        load.start()

    barrier = pltpu.get_barrier_semaphore()
    others = [o for o in range(-RANGE, RANGE + 1) if o != 0]
    greeted = others + [-8, 8]
    for o in greeted:
        pl.semaphore_signal(barrier, inc=1, device_id=device(me + o), device_id_type=MESH)
    bbuf[OWN] = bias_ref[...]
    for load in loads:
        load.wait()
    pl.semaphore_wait(barrier, len(greeted))

    def put(src, dst, to, sent, got):
        return pltpu.make_async_remote_copy(
            src_ref=src, dst_ref=dst, send_sem=sent, recv_sem=got, device_id=to, device_id_type=MESH
        )

    def piece(slot, m, h, to, to_slot, n):
        return put(buf.at[slot, m, h], buf.at[to_slot, m, h], to, send_sem.at[n], recv_sem.at[to_slot, m, h])

    def arrival(slot, m, h):
        return piece(slot, m, h, sibling, slot, 0)

    def bias_copy(o):
        slot = OWN - o
        return put(bbuf.at[OWN], bbuf.at[slot], device(me + o), bsend.at[OWN + o], brecv.at[slot])

    def bias_arrival(slot):
        return put(bbuf.at[slot], bbuf.at[slot], sibling, bsend.at[0], brecv.at[slot])

    def lse_copy(o):
        slot = OWN - o
        return put(lbuf.at[OWN], lbuf.at[slot], device(me + o), lsend.at[OWN + o], lrecv.at[slot])

    def choose(a, b):
        return tuple(jnp.where(corner, u, v) for u, v in zip(a, b))

    x_out = [
        choose((OWN, 1, at(-tau)), (OWN, j - 1, at(-tau))),
        choose((OWN, 0, at(-tau)), (OWN, 2 - j, at(-tau))),
        choose((ys, across, at(sigma)), (zs, 0, at(-sigma))),
    ]
    y_out = [
        choose((OWN, 0, at(-2 * sigma)), (OWN, 2 - j, at(-2 * sigma))),
        choose((OWN, 1, at(-2 * sigma)), (xs, 1, PASSING)),
        choose((xs, across, at(-sigma)), (OWN, j - 1, at(-2 * sigma))),
    ]
    x_in = [
        choose((xs, across), (xs, 1)),
        choose((xs, 1 - across), (xs, 0)),
        choose((fs, 0), (fs, j - 1)),
    ]
    y_in = [
        choose((ys, across), (ys, 0)),
        choose((PASSING, 1), (ys, 1)),
        choose((ys, 1 - across), (fs, 2 - j)),
    ]
    z_in = [
        choose((zs, across), (zs, 0)),
        choose((fs, 1), (zs, 1)),
        choose((zs, 1 - across), (zs, 1)),
    ]

    def pick(groups, i):
        g = i // 2
        return tuple(jnp.where(g == 0, a, jnp.where(g == 1, b, c)) for a, b, c in zip(*groups))

    def x_send(i):
        slot, m, there = pick(x_out, i)
        return piece(slot, m, i % 2, x_dev, there, i)

    def y_send(i):
        slot, m, there = pick(y_out, i)
        return piece(slot, m, i % 2, y_dev, there, 6 + i)

    def z_send(i):
        slot, m = pick(y_in, i)
        there = jnp.where(slot == PASSING, at(-sigma), at(-2 * sigma))
        return piece(slot, m, i % 2, z_dev, there, 12 + i)

    def z_count():
        return jnp.where(corner, 6, 4)

    def shared(slot, step):
        there = slot + step
        return jnp.logical_and(jnp.logical_and(there >= 0, there < SLOTS), slot != PASSING)

    def forward(groups, i, n):
        slot, m = pick(groups, i)
        return shared(slot, -turn), piece(slot, m, i % 2, sibling, jnp.where(shared(slot, -turn), slot - turn, 0), n + i)

    for i in range(2):
        x_send(i).start()
        y_send(i).start()
    for o in others:
        bias_copy(o).start()
    own_s = [piece(OWN, m, h, sibling, OWN - turn, 36 + 2 * m + h) for m in range(2) for h in range(2)]
    for copy in own_s:
        copy.start()

    tops[...] = jnp.full(tops.shape, FAR, jnp.float32)
    totals[...] = jnp.zeros(totals.shape, jnp.float32)

    def score(slot, m, h):
        side = 1 - m
        bias = bbuf[jnp.where(side == 0, OWN, slot), pl.ds(jnp.where(side == 0, slot, SLOTS - 1 - slot), 1), :]
        bias = bias[:, :half]
        right = buf[slot, m, h]
        for r in range(2):
            part = pl.ds(r * half, half)
            s = SCALE * lax.dot_general(
                buf[OWN, side, r], right, NT, preferred_element_type=jnp.float32
            ) + bias
            sc[slot, side, h, part, :] = s
            old = tops[side, part, :]
            top = jnp.maximum(old, jnp.max(s, axis=1, keepdims=True))
            total = totals[side, part, :] * jnp.exp(old - top)
            totals[side, part, :] = total + jnp.sum(jnp.exp(s - top), axis=1, keepdims=True)
            tops[side, part, :] = top

    def own(e, carry):
        score(OWN, e // 2, e % 2)
        return carry

    def beside(e, carry):
        arrival(OWN + turn, e // 2, e % 2).wait_recv()
        score(OWN + turn, e // 2, e % 2)
        return carry

    lax.fori_loop(0, 4, own, 0)
    for o in others:
        bias_arrival(OWN - o).wait_recv()
    lax.fori_loop(0, 4, beside, 0)

    def step(t, carry):
        @pl.when(t < 6)
        def _():
            slot, m = pick(x_in, t)
            arrival(slot, m, t % 2).wait_recv()

            @pl.when(t < 4)
            def _():
                x_send(t + 2).start()

            slot, m = pick(y_in, t)
            arrival(slot, m, t % 2).wait_recv()

            @pl.when(t < z_count())
            def _():
                z_send(t).start()

            @pl.when(t < 4)
            def _():
                y_send(t + 2).start()

            for groups, n in ((x_in, 18), (y_in, 24)):
                used, copy = forward(groups, t, n)

                @pl.when(used)
                def _():
                    copy.start()

        @pl.when(jnp.logical_and(t >= 1, t - 1 < z_count()))
        def _():
            slot, m = pick(z_in, t - 1)
            arrival(slot, m, (t - 1) % 2).wait_recv()
            used, copy = forward(z_in, t - 1, 30)

            @pl.when(used)
            def _():
                copy.start()

        def sub(u, carry):
            link = u % 3
            beside = u // 3
            i = t - beside - jnp.where(link == 2, 1, 0)
            near = jnp.logical_and(i >= 0, i < jnp.where(link == 2, z_count(), 6))
            i = jnp.where(near, i, 0)
            slot, m = (
                jnp.where(link == 0, a, jnp.where(link == 1, b, c))
                for a, b, c in zip(pick(x_in, i), pick(y_in, i), pick(z_in, i))
            )
            moved = jnp.where(beside == 1, turn, 0)
            near = jnp.logical_and(near, shared(slot, moved))
            slot = jnp.where(near, slot + moved, 0)

            @pl.when(near)
            def _():
                @pl.when(beside == 1)
                def _():
                    arrival(slot, m, i % 2).wait_recv()

                score(slot, m, i % 2)

            return carry

        lax.fori_loop(0, 6, sub, 0)
        return carry

    lax.fori_loop(0, 8, step, 0)

    for side in range(2):
        lse = tops[side] + jnp.log(totals[side])
        tops[side] = lse
        lbuf[OWN, side] = jnp.transpose(jnp.broadcast_to(lse, (rows, 128)))[0:8]
    for o in others:
        lse_copy(o).start()

    grads = (gq_ref, gp_ref)

    def weight(slot, side, part):
        s = jnp.concatenate([sc[slot, side, h, part, :] for h in range(2)], axis=1)
        w = jnp.exp(s - tops[side, part, :]) + jnp.exp(s - lbuf[slot, 1 - side, 0:1, :])
        return s, w

    def product(w, slot, side):
        right = buf[slot, 1 - side].reshape(rows, buf.shape[4])
        return jnp.dot((SCALE * w).astype(jnp.bfloat16), right, preferred_element_type=jnp.float32)

    for side in range(2):
        for r in range(0, rows, half):
            part = pl.ds(r, half)
            s, w = weight(OWN, side, part)
            if side == 0:
                hit = pos_col[part, :] == lax.broadcasted_iota(jnp.int32, s.shape, 1)
            else:
                hit = pos_row[...] == lax.broadcasted_iota(jnp.int32, s.shape, 0) + r
            e = hit.astype(jnp.float32)
            totals[side, part, :] = tops[side, part, :] - jnp.sum(s * e, axis=1, keepdims=True)
            grads[side][part, :] = product(w - 2.0 * e, OWN, side)
        loss_ref[side] = jnp.transpose(jnp.broadcast_to(totals[side], (rows, 128)))[0:8]

    def later(t, carry):
        pair = (t, SLOTS - 1 - t)
        for slot in pair:
            put(lbuf.at[slot], lbuf.at[slot], sibling, lsend.at[0], lrecv.at[slot]).wait_recv()
        for side in range(2):
            for r in range(0, rows, half):
                part = pl.ds(r, half)
                terms = [product(weight(slot, side, part)[1], slot, side) for slot in pair]
                grads[side][part, :] += terms[0] + terms[1]
        return carry

    lax.fori_loop(0, RANGE, later, 0)

    for copy in own_s:
        copy.wait_send()

    def sent(i, carry):
        x_send(i).wait_send()
        y_send(i).wait_send()
        for groups, n, count in ((x_in, 18, 6), (y_in, 24, 6), (z_in, 30, z_count())):
            used, copy = forward(groups, i, n)

            @pl.when(jnp.logical_and(used, i < count))
            def _():
                copy.wait_send()

        @pl.when(i < z_count())
        def _():
            z_send(i).wait_send()

        return carry

    lax.fori_loop(0, 6, sent, 0)
    for o in others:
        bias_copy(o).wait_send()
        lse_copy(o).wait_send()


def present_pairs(pair_blocks, negative_pair_count, block, blocks):
    listed = pair_blocks.shape[1]
    used = jnp.arange(listed, dtype=jnp.int32) < negative_pair_count[0]
    offsets = jnp.arange(-RANGE, RANGE + 1, dtype=jnp.int32)
    target = (block + offsets) % blocks
    found = jnp.any((pair_blocks[0][None, :] == target[:, None]) & used[None, :], axis=1)
    return found | (offsets == 0)


def solution(mesh):
    chips = mesh.shape["dp"]
    blocks = chips * mesh.shape["cores"]

    def body(queries, passages, positives, pair_blocks, negative_pair_count):
        rows, width = queries.shape
        block = lax.axis_index(("dp", "cores"))
        present = present_pairs(pair_blocks, negative_pair_count, block, blocks)
        bias = jnp.where(present, 0.0, FAR).astype(jnp.float32)
        bias = jnp.broadcast_to(jnp.pad(bias, (0, 16 - SLOTS))[:, None], (16, rows))
        vmem = pl.BlockSpec(memory_space=pltpu.VMEM)
        anywhere = pl.BlockSpec(memory_space=pl.ANY)
        gq, gp, loss = pl.pallas_call(
            functools.partial(kernel, chips),
            out_shape=(
                jax.ShapeDtypeStruct((rows, width), jnp.float32),
                jax.ShapeDtypeStruct((rows, width), jnp.float32),
                jax.ShapeDtypeStruct((2, 8, rows), jnp.float32),
            ),
            in_specs=[anywhere, anywhere, vmem, vmem, vmem],
            out_specs=(vmem, vmem, vmem),
            scratch_shapes=[
                pltpu.VMEM((SLOTS + 1, 2, 2, rows // 2, width), jnp.bfloat16),
                pltpu.VMEM((SLOTS, 2, 2, rows, rows // 2), jnp.float32),
                pltpu.VMEM((2, rows, 1), jnp.float32),
                pltpu.VMEM((2, rows, 1), jnp.float32),
                pltpu.VMEM((SLOTS, 16, rows), jnp.float32),
                pltpu.VMEM((SLOTS, 2, 8, rows), jnp.float32),
                pltpu.SemaphoreType.DMA((4,)),
                pltpu.SemaphoreType.DMA((40,)),
                pltpu.SemaphoreType.DMA((SLOTS + 1, 2, 2)),
                pltpu.SemaphoreType.DMA((SLOTS,)),
                pltpu.SemaphoreType.DMA((SLOTS,)),
                pltpu.SemaphoreType.DMA((SLOTS,)),
                pltpu.SemaphoreType.DMA((SLOTS,)),
            ],
            compiler_params=pltpu.CompilerParams(
                collective_id=0, has_side_effects=True, vmem_limit_bytes=58 * 2**20
            ),
            cost_estimate=pl.CostEstimate(
                flops=36 * 2 * rows * rows * width,
                bytes_accessed=12 * rows * width,
                transcendentals=54 * rows * rows,
            ),
        )(queries, passages, bias, positives.reshape(rows, 1), positives)
        return loss[0, 0:1], loss[1, 0:1], gq, gp

    split = P(("dp", "cores"), None)
    return jax.shard_map(
        body,
        mesh=mesh,
        in_specs=(split, split, split, split, P(("dp", "cores"))),
        out_specs=(split, split, split, split),
        check_vma=False,
    )
```

time: 140 us -> 140 us (level)
  no operation moved by 1% of the time
where the time goes in v2:
time: 140 us; the launch traced here: 138 us
  Pallas kernels  128 us (91%)
  local copies, waits for them, and re-layouts  8.18 us (6%)
    pallas_call x1, Pallas kernels, body(): pl.pallas_call(functools.partial(kernel, chips), out_shape=(jax.ShapeDtyp...  128 us
    unnamed x4, local copies, waits for them, and re-layouts  4.63 us

profile of v2, /device:TPU:0, one launch (start us, length us, event | category | flops | bytes accessed | tf_op | source)
XLA Modules:
  0.0 138.4 jit_solution(8499456044930359863)
XLA Ops:
  1.3 0.7 and_reduce_fusion
  2.1 0.7 broadcast_in_dim.18.bias_ref
  2.8 1.5 %copy.10.pos_col = s32[512,1]{1,0:T(8,128)} copy(s32[512,1]{0,1:T(1,128)} %bitcast.8) | data formatting | bytes 4096 | tf_op jit(solution)/shard_map/reshape | solution.py:380
  4.3 128.1 %shard_map.84 = (f32[512,1024]{1,0:T(8,128)}, f32[512,1024]{1,0:T(8,128)}, f32[2,8,512]{2,1,0:T(8,128)}) custom-call(bf16[512,1024]{1,0:T(8,128)(2,1)} %q_hbm.1, bf16[512,1024]{1,0:T(8,128)(2,1)} %p_hbm.1, f32[16,512]{1,0:T(8,128)} %broadcast_in_dim.18.bias_ref, s32[512,1]{1,0:T(8,128)} %copy.10.pos_col, s32[1,512]{1,0:T(1,128)} %pos_row.1), custom_call_target="tpu_custom_call" | custom-call | flops 19327352832 | bytes 6291456 | tf_op jit(solution)/shard_map/pallas_call | solution.py:348
  132.4 1.3 slice_bitcast_fusion
  133.8 0.0 copy-start
  133.8 3.3 %copy.14 = f32[512,1024]{1,0:T(8,128)} copy(f32[512,1024]{1,0:T(8,128)} %get-tuple-element.18) | data formatting | bytes 4194304
  137.1 0.0 copy-done
  137.1 1.3 copy.15
  (4 shorter events, 0.0 us)
Async XLA Ops:
  133.8 3.3 %copy-start = (f32[512,1024]{1,0:T(8,128)S(1)}, f32[512,1024]{1,0:T(8,128)}, u32[]{:S(2)}) copy-start(f32[512,1024]{1,0:T(8,128)} %get-tuple-element.19) | copy-start | bytes 6291460

commit v3 on v2

--- a/solution.py
+++ b/solution.py
@@ -13,13 +13,15 @@
 PASSING = SLOTS
 MESH = pl.DeviceIdType.MESH
 SCALE = 20.0
+LOG2E = 1.4426950408889634
+LOG2_SCALE = 4.321928094887363
 FAR = -1.0e30
 
 NT = (((1,), (1,)), ((), ()))
 
 
-def kernel(chips, q_hbm, p_hbm, bias_ref, pos_col, pos_row, gq_ref, gp_ref, loss_ref,
-           buf, sc, tops, totals, bbuf, lbuf,
+def kernel(chips, q_hbm, p_hbm, bias_ref, pos_row, gq_ref, gp_ref, loss_ref,
+           buf, sc, weights, tops, totals, bbuf, lbuf,
            load_sem, send_sem, recv_sem, bsend, brecv, lsend, lrecv):
     chip = lax.axis_index("dp")
     core = lax.axis_index("cores")
@@ -52,7 +54,7 @@
     for m, ref in enumerate((q_hbm, p_hbm)):
         for h in range(2):
             loads.append(pltpu.make_async_copy(
-                ref.at[pl.ds(h * half, half)], buf.at[OWN, m, h], load_sem.at[2 * m + h]))
+                ref.at[pl.ds(h * half, half)], buf.at[m, OWN, h], load_sem.at[2 * m + h]))
     for load in loads:
         load.start()
 
@@ -72,7 +74,7 @@
         )
 
     def piece(slot, m, h, to, to_slot, n):
-        return put(buf.at[slot, m, h], buf.at[to_slot, m, h], to, send_sem.at[n], recv_sem.at[to_slot, m, h])
+        return put(buf.at[m, slot, h], buf.at[m, to_slot, h], to, send_sem.at[n], recv_sem.at[to_slot, m, h])
 
     def arrival(slot, m, h):
         return piece(slot, m, h, sibling, slot, 0)
@@ -161,18 +163,15 @@
         side = 1 - m
         bias = bbuf[jnp.where(side == 0, OWN, slot), pl.ds(jnp.where(side == 0, slot, SLOTS - 1 - slot), 1), :]
         bias = bias[:, :half]
-        right = buf[slot, m, h]
-        for r in range(2):
-            part = pl.ds(r * half, half)
-            s = SCALE * lax.dot_general(
-                buf[OWN, side, r], right, NT, preferred_element_type=jnp.float32
-            ) + bias
-            sc[slot, side, h, part, :] = s
-            old = tops[side, part, :]
-            top = jnp.maximum(old, jnp.max(s, axis=1, keepdims=True))
-            total = totals[side, part, :] * jnp.exp(old - top)
-            totals[side, part, :] = total + jnp.sum(jnp.exp(s - top), axis=1, keepdims=True)
-            tops[side, part, :] = top
+        left = buf[side, OWN].reshape(rows, buf.shape[4])
+        s = (SCALE * LOG2E) * lax.dot_general(
+            left, buf[m, slot, h], NT, preferred_element_type=jnp.float32
+        ) + bias
+        sc[slot, side, h] = s
+        old = tops[side]
+        top = jnp.maximum(old, jnp.max(s, axis=1, keepdims=True))
+        totals[side] = totals[side] * jnp.exp2(old - top) + jnp.sum(jnp.exp2(s - top), axis=1, keepdims=True)
+        tops[side] = top
 
     def own(e, carry):
         score(OWN, e // 2, e % 2)
@@ -256,48 +255,65 @@
     lax.fori_loop(0, 8, step, 0)
 
     for side in range(2):
-        lse = tops[side] + jnp.log(totals[side])
+        lse = tops[side] + jnp.log2(totals[side]) - LOG2_SCALE
         tops[side] = lse
         lbuf[OWN, side] = jnp.transpose(jnp.broadcast_to(lse, (rows, 128)))[0:8]
     for o in others:
         lse_copy(o).start()
 
-    grads = (gq_ref, gp_ref)
-
-    def weight(slot, side, part):
-        s = jnp.concatenate([sc[slot, side, h, part, :] for h in range(2)], axis=1)
-        w = jnp.exp(s - tops[side, part, :]) + jnp.exp(s - lbuf[slot, 1 - side, 0:1, :])
-        return s, w
-
-    def product(w, slot, side):
-        right = buf[slot, 1 - side].reshape(rows, buf.shape[4])
-        return jnp.dot((SCALE * w).astype(jnp.bfloat16), right, preferred_element_type=jnp.float32)
-
+    def columns(start, size):
+        return pl.ds(start if isinstance(start, int) else pl.multiple_of(start, 128), size)
+
+    def weigh(slot, side):
+        for h in range(2):
+            s = sc[slot, side, h]
+            w = jnp.exp2(s - tops[side]) + jnp.exp2(s - lbuf[slot, 1 - side, 0:1, pl.ds(h * half, half)])
+            weights[side, :, columns(slot * rows + h * half, half)] = w.astype(jnp.bfloat16)
+
+    pos_col = jnp.transpose(jnp.broadcast_to(pos_row[...].astype(jnp.float32), (128, rows)))[:, 0:1].astype(jnp.int32)
     for side in range(2):
-        for r in range(0, rows, half):
-            part = pl.ds(r, half)
-            s, w = weight(OWN, side, part)
+        paired = jnp.zeros((rows, 1), jnp.float32)
+        for h in range(2):
+            s = sc[OWN, side, h]
+            part = pl.ds(h * half, half)
             if side == 0:
-                hit = pos_col[part, :] == lax.broadcasted_iota(jnp.int32, s.shape, 1)
+                hit = pos_col == lax.broadcasted_iota(jnp.int32, s.shape, 1) + h * half
             else:
-                hit = pos_row[...] == lax.broadcasted_iota(jnp.int32, s.shape, 0) + r
+                hit = pos_row[:, part] == lax.broadcasted_iota(jnp.int32, s.shape, 0)
             e = hit.astype(jnp.float32)
-            totals[side, part, :] = tops[side, part, :] - jnp.sum(s * e, axis=1, keepdims=True)
-            grads[side][part, :] = product(w - 2.0 * e, OWN, side)
-        loss_ref[side] = jnp.transpose(jnp.broadcast_to(totals[side], (rows, 128)))[0:8]
-
-    def later(t, carry):
-        pair = (t, SLOTS - 1 - t)
-        for slot in pair:
-            put(lbuf.at[slot], lbuf.at[slot], sibling, lsend.at[0], lrecv.at[slot]).wait_recv()
-        for side in range(2):
-            for r in range(0, rows, half):
-                part = pl.ds(r, half)
-                terms = [product(weight(slot, side, part)[1], slot, side) for slot in pair]
-                grads[side][part, :] += terms[0] + terms[1]
-        return carry
-
-    lax.fori_loop(0, RANGE, later, 0)
+            paired = paired + jnp.sum(s * e, axis=1, keepdims=True)
+            w = jnp.exp2(s - tops[side]) + jnp.exp2(s - lbuf[OWN, 1 - side, 0:1, part])
+            weights[side, :, columns(OWN * rows + h * half, half)] = (w - 2.0 * SCALE * e).astype(jnp.bfloat16)
+        loss = (tops[side] + LOG2_SCALE - paired) / LOG2E
+        loss_ref[side] = jnp.transpose(jnp.broadcast_to(loss, (rows, 128)))[0:8]
+
+    for o in others:
+        put(lbuf.at[OWN - o], lbuf.at[OWN - o], sibling, lsend.at[0], lrecv.at[OWN - o]).wait_recv()
+
+    def product(side, n):
+        cols = columns(n * half, half)
+        right = buf[1 - side, pl.ds(0, SLOTS), :, :, cols].reshape(SLOTS * rows, half)
+        ref = (gq_ref, gp_ref)[side]
+        ref[:, cols] = jnp.dot(weights[side], right, preferred_element_type=jnp.float32)
+
+    def first(t, carry):
+        weigh(t + t // RANGE, 0)
+        return carry
+
+    def both(n, carry):
+        product(0, n)
+        for t in range(2):
+            t = 2 * n + t
+            weigh(t + t // RANGE, 1)
+        return carry
+
+    def second(n, carry):
+        product(1, n)
+        return carry
+
+    lax.fori_loop(0, SLOTS - 1, first, 0)
+    lax.fori_loop(0, 4, both, 0)
+    lax.fori_loop(0, 4, second, 0)
 
     for copy in own_s:
         copy.wait_send()
@@ -352,11 +368,12 @@
                 jax.ShapeDtypeStruct((rows, width), jnp.float32),
                 jax.ShapeDtypeStruct((2, 8, rows), jnp.float32),
             ),
-            in_specs=[anywhere, anywhere, vmem, vmem, vmem],
+            in_specs=[anywhere, anywhere, vmem, vmem],
             out_specs=(vmem, vmem, vmem),
             scratch_shapes=[
-                pltpu.VMEM((SLOTS + 1, 2, 2, rows // 2, width), jnp.bfloat16),
+                pltpu.VMEM((2, SLOTS + 1, 2, rows // 2, width), jnp.bfloat16),
                 pltpu.VMEM((SLOTS, 2, 2, rows, rows // 2), jnp.float32),
+                pltpu.VMEM((2, rows, SLOTS * rows), jnp.bfloat16),
                 pltpu.VMEM((2, rows, 1), jnp.float32),
                 pltpu.VMEM((2, rows, 1), jnp.float32),
                 pltpu.VMEM((SLOTS, 16, rows), jnp.float32),
@@ -370,14 +387,14 @@
                 pltpu.SemaphoreType.DMA((SLOTS,)),
             ],
             compiler_params=pltpu.CompilerParams(
-                collective_id=0, has_side_effects=True, vmem_limit_bytes=58 * 2**20
+                collective_id=0, has_side_effects=True, vmem_limit_bytes=60 * 2**20
             ),
             cost_estimate=pl.CostEstimate(
                 flops=36 * 2 * rows * rows * width,
                 bytes_accessed=12 * rows * width,
                 transcendentals=54 * rows * rows,
             ),
-        )(queries, passages, bias, positives.reshape(rows, 1), positives)
+        )(queries, passages, bias, positives)
         return loss[0, 0:1], loss[1, 0:1], gq, gp
 
     split = P(("dp", "cores"), None)

time: 140 us -> 146 us (1.043); the launches traced: 138 us -> 146 us
  Pallas kernels: 128 us -> 137 us
  local copies, waits for them, and re-layouts: 8.18 us -> 6.64 us
    pallas_call x1, Pallas kernels: 128 us -> 137 us  [body(): pl.pallas_call(functools.partial(kernel, chips), out_shape=(jax.ShapeDtyp...]
    reshape x1 -> x0, local copies, waits for them, and re-layouts: 1.53 us -> none  [body(): positives.reshape(rows, 1)]
where the time goes in v3:
time: 146 us
  Pallas kernels  137 us (94%)
  local copies, waits for them, and re-layouts  6.64 us (5%)
    pallas_call x1, Pallas kernels, body(): pl.pallas_call(functools.partial(kernel, chips), out_shape=(jax.ShapeDtyp...  137 us
    unnamed x4, local copies, waits for them, and re-layouts  4.63 us

profile of v3, /device:TPU:0, one launch (start us, length us, event | category | flops | bytes accessed | tf_op | source)
XLA Modules:
  0.0 146.1 jit_solution(2456523017256162710)
XLA Ops:
  1.3 0.7 and_reduce_fusion
  2.1 0.7 broadcast_in_dim.18.bias_ref
  2.8 137.3 %shard_map.84 = (f32[512,1024]{1,0:T(8,128)}, f32[512,1024]{1,0:T(8,128)}, f32[2,8,512]{2,1,0:T(8,128)}) custom-call(bf16[512,1024]{1,0:T(8,128)(2,1)} %q_hbm.1, bf16[512,1024]{1,0:T(8,128)(2,1)} %p_hbm.1, f32[16,512]{1,0:T(8,128)} %broadcast_in_dim.18.bias_ref, s32[1,512]{1,0:T(1,128)} %pos_row.1), custom_call_target="tpu_custom_call" | custom-call | flops 19327352832 | bytes 6291456 | tf_op jit(solution)/shard_map/pallas_call | solution.py:364
  140.1 1.3 slice_bitcast_fusion
  141.4 0.0 copy-start
  141.4 3.3 %copy.12 = f32[512,1024]{1,0:T(8,128)} copy(f32[512,1024]{1,0:T(8,128)} %get-tuple-element.18) | data formatting | bytes 4194304
  144.7 0.0 copy-done
  144.7 1.3 copy.13
  (4 shorter events, 0.0 us)
Async XLA Ops:
  141.4 3.3 %copy-start = (f32[512,1024]{1,0:T(8,128)S(1)}, f32[512,1024]{1,0:T(8,128)}, u32[]{:S(2)}) copy-start(f32[512,1024]{1,0:T(8,128)} %get-tuple-element.19) | copy-start | bytes 6291460

commit v4 on v2

--- a/solution.py
+++ b/solution.py
@@ -12,13 +12,16 @@
 SLOTS = 2 * RANGE + 1
 PASSING = SLOTS
 MESH = pl.DeviceIdType.MESH
+LANES = 128
 SCALE = 20.0
+LOG2E = 1.4426950408889634
+LOG2_SCALE = 4.321928094887363
 FAR = -1.0e30
 
 NT = (((1,), (1,)), ((), ()))
 
 
-def kernel(chips, q_hbm, p_hbm, bias_ref, pos_col, pos_row, gq_ref, gp_ref, loss_ref,
+def kernel(chips, q_hbm, p_hbm, bias_ref, pos_row, gq_ref, gp_ref, loss_ref,
            buf, sc, tops, totals, bbuf, lbuf,
            load_sem, send_sem, recv_sem, bsend, brecv, lsend, lrecv):
     chip = lax.axis_index("dp")
@@ -52,7 +55,7 @@
     for m, ref in enumerate((q_hbm, p_hbm)):
         for h in range(2):
             loads.append(pltpu.make_async_copy(
-                ref.at[pl.ds(h * half, half)], buf.at[OWN, m, h], load_sem.at[2 * m + h]))
+                ref.at[pl.ds(h * half, half)], buf.at[m, OWN, h], load_sem.at[2 * m + h]))
     for load in loads:
         load.start()
 
@@ -72,7 +75,7 @@
         )
 
     def piece(slot, m, h, to, to_slot, n):
-        return put(buf.at[slot, m, h], buf.at[to_slot, m, h], to, send_sem.at[n], recv_sem.at[to_slot, m, h])
+        return put(buf.at[m, slot, h], buf.at[m, to_slot, h], to, send_sem.at[n], recv_sem.at[to_slot, m, h])
 
     def arrival(slot, m, h):
         return piece(slot, m, h, sibling, slot, 0)
@@ -161,17 +164,18 @@
         side = 1 - m
         bias = bbuf[jnp.where(side == 0, OWN, slot), pl.ds(jnp.where(side == 0, slot, SLOTS - 1 - slot), 1), :]
         bias = bias[:, :half]
-        right = buf[slot, m, h]
+        right = buf[m, slot, h]
         for r in range(2):
             part = pl.ds(r * half, half)
-            s = SCALE * lax.dot_general(
-                buf[OWN, side, r], right, NT, preferred_element_type=jnp.float32
+            s = (SCALE * LOG2E) * lax.dot_general(
+                buf[side, OWN, r], right, NT, preferred_element_type=jnp.float32
             ) + bias
             sc[slot, side, h, part, :] = s
+            groups = [s[:, c:c + LANES] for c in range(0, half, LANES)]
             old = tops[side, part, :]
-            top = jnp.maximum(old, jnp.max(s, axis=1, keepdims=True))
-            total = totals[side, part, :] * jnp.exp(old - top)
-            totals[side, part, :] = total + jnp.sum(jnp.exp(s - top), axis=1, keepdims=True)
+            top = functools.reduce(jnp.maximum, groups, old)
+            total = totals[side, part, :] * jnp.exp2(old - top)
+            totals[side, part, :] = sum((jnp.exp2(g - top) for g in groups), total)
             tops[side, part, :] = top
 
     def own(e, carry):
@@ -256,9 +260,11 @@
     lax.fori_loop(0, 8, step, 0)
 
     for side in range(2):
-        lse = tops[side] + jnp.log(totals[side])
+        top = jnp.max(tops[side], axis=1, keepdims=True)
+        total = jnp.sum(totals[side] * jnp.exp2(tops[side] - top), axis=1, keepdims=True)
+        lse = jnp.broadcast_to(top + jnp.log2(total) - LOG2_SCALE, (rows, LANES))
         tops[side] = lse
-        lbuf[OWN, side] = jnp.transpose(jnp.broadcast_to(lse, (rows, 128)))[0:8]
+        lbuf[OWN, side] = jnp.transpose(lse)[0:8]
     for o in others:
         lse_copy(o).start()
 
@@ -266,25 +272,27 @@
 
     def weight(slot, side, part):
         s = jnp.concatenate([sc[slot, side, h, part, :] for h in range(2)], axis=1)
-        w = jnp.exp(s - tops[side, part, :]) + jnp.exp(s - lbuf[slot, 1 - side, 0:1, :])
-        return s, w
+        lse = jnp.concatenate([tops[side, part, :]] * (rows // LANES), axis=1)
+        return s, jnp.exp2(s - lse) + jnp.exp2(s - lbuf[slot, 1 - side, 0:1, :])
 
     def product(w, slot, side):
-        right = buf[slot, 1 - side].reshape(rows, buf.shape[4])
-        return jnp.dot((SCALE * w).astype(jnp.bfloat16), right, preferred_element_type=jnp.float32)
-
+        right = buf[1 - side, slot].reshape(rows, buf.shape[4])
+        return jnp.dot(w.astype(jnp.bfloat16), right, preferred_element_type=jnp.float32)
+
+    pos_col = jnp.transpose(jnp.broadcast_to(pos_row[...].astype(jnp.float32), (LANES, rows)))[:, 0:1].astype(jnp.int32)
     for side in range(2):
         for r in range(0, rows, half):
             part = pl.ds(r, half)
             s, w = weight(OWN, side, part)
             if side == 0:
-                hit = pos_col[part, :] == lax.broadcasted_iota(jnp.int32, s.shape, 1)
+                hit = pos_col[r:r + half] == lax.broadcasted_iota(jnp.int32, s.shape, 1)
             else:
                 hit = pos_row[...] == lax.broadcasted_iota(jnp.int32, s.shape, 0) + r
             e = hit.astype(jnp.float32)
-            totals[side, part, :] = tops[side, part, :] - jnp.sum(s * e, axis=1, keepdims=True)
-            grads[side][part, :] = product(w - 2.0 * e, OWN, side)
-        loss_ref[side] = jnp.transpose(jnp.broadcast_to(totals[side], (rows, 128)))[0:8]
+            paired = jnp.sum(s * e, axis=1, keepdims=True)
+            totals[side, part, :] = (tops[side, part, :] + LOG2_SCALE - paired) / LOG2E
+            grads[side][part, :] = product(w - 2.0 * SCALE * e, OWN, side)
+        loss_ref[side] = jnp.transpose(totals[side])[0:8]
 
     def later(t, carry):
         pair = (t, SLOTS - 1 - t)
@@ -352,13 +360,13 @@
                 jax.ShapeDtypeStruct((rows, width), jnp.float32),
                 jax.ShapeDtypeStruct((2, 8, rows), jnp.float32),
             ),
-            in_specs=[anywhere, anywhere, vmem, vmem, vmem],
+            in_specs=[anywhere, anywhere, vmem, vmem],
             out_specs=(vmem, vmem, vmem),
             scratch_shapes=[
-                pltpu.VMEM((SLOTS + 1, 2, 2, rows // 2, width), jnp.bfloat16),
+                pltpu.VMEM((2, SLOTS + 1, 2, rows // 2, width), jnp.bfloat16),
                 pltpu.VMEM((SLOTS, 2, 2, rows, rows // 2), jnp.float32),
-                pltpu.VMEM((2, rows, 1), jnp.float32),
-                pltpu.VMEM((2, rows, 1), jnp.float32),
+                pltpu.VMEM((2, rows, LANES), jnp.float32),
+                pltpu.VMEM((2, rows, LANES), jnp.float32),
                 pltpu.VMEM((SLOTS, 16, rows), jnp.float32),
                 pltpu.VMEM((SLOTS, 2, 8, rows), jnp.float32),
                 pltpu.SemaphoreType.DMA((4,)),
@@ -370,14 +378,14 @@
                 pltpu.SemaphoreType.DMA((SLOTS,)),
             ],
             compiler_params=pltpu.CompilerParams(
-                collective_id=0, has_side_effects=True, vmem_limit_bytes=58 * 2**20
+                collective_id=0, has_side_effects=True, vmem_limit_bytes=60 * 2**20
             ),
             cost_estimate=pl.CostEstimate(
                 flops=36 * 2 * rows * rows * width,
                 bytes_accessed=12 * rows * width,
                 transcendentals=54 * rows * rows,
             ),
-        )(queries, passages, bias, positives.reshape(rows, 1), positives)
+        )(queries, passages, bias, positives)
         return loss[0, 0:1], loss[1, 0:1], gq, gp
 
     split = P(("dp", "cores"), None)

time: 140 us -> 135 us (0.964)
  Pallas kernels: 128 us -> 124 us
  local copies, waits for them, and re-layouts: 8.18 us -> 6.64 us
    pallas_call x1, Pallas kernels: 128 us -> 124 us  [body(): pl.pallas_call(functools.partial(kernel, chips), out_shape=(jax.ShapeDtyp...]
    reshape x1 -> x0, local copies, waits for them, and re-layouts: 1.53 us -> none  [body(): positives.reshape(rows, 1)]
where the time goes in v4:
time: 135 us; the launch traced here: 133 us
  Pallas kernels  124 us (92%)
  local copies, waits for them, and re-layouts  6.64 us (5%)
    pallas_call x1, Pallas kernels, body(): pl.pallas_call(functools.partial(kernel, chips), out_shape=(jax.ShapeDtyp...  124 us
    unnamed x4, local copies, waits for them, and re-layouts  4.63 us

profile of v4, /device:TPU:0, one launch (start us, length us, event | category | flops | bytes accessed | tf_op | source)
XLA Modules:
  0.0 132.5 jit_solution(17923458396845957769)
XLA Ops:
  1.3 0.7 and_reduce_fusion
  2.1 0.7 broadcast_in_dim.18.bias_ref
  2.8 123.8 %shard_map.84 = (f32[512,1024]{1,0:T(8,128)}, f32[512,1024]{1,0:T(8,128)}, f32[2,8,512]{2,1,0:T(8,128)}) custom-call(bf16[512,1024]{1,0:T(8,128)(2,1)} %q_hbm.1, bf16[512,1024]{1,0:T(8,128)(2,1)} %p_hbm.1, f32[16,512]{1,0:T(8,128)} %broadcast_in_dim.18.bias_ref, s32[1,512]{1,0:T(1,128)} %pos_row.1), custom_call_target="tpu_custom_call" | custom-call | flops 19327352832 | bytes 6291456 | tf_op jit(solution)/shard_map/pallas_call | solution.py:356
  126.6 1.3 slice_bitcast_fusion
  127.9 0.0 copy-start
  127.9 3.3 %copy.12 = f32[512,1024]{1,0:T(8,128)} copy(f32[512,1024]{1,0:T(8,128)} %get-tuple-element.18) | data formatting | bytes 4194304
  131.2 0.0 copy-done
  131.2 1.3 copy.13
  (4 shorter events, 0.0 us)
Async XLA Ops:
  127.9 3.3 %copy-start = (f32[512,1024]{1,0:T(8,128)S(1)}, f32[512,1024]{1,0:T(8,128)}, u32[]{:S(2)}) copy-start(f32[512,1024]{1,0:T(8,128)} %get-tuple-element.19) | copy-start | bytes 6291460

commit v5 on v4

--- a/solution.py
+++ b/solution.py
@@ -164,13 +164,14 @@
         side = 1 - m
         bias = bbuf[jnp.where(side == 0, OWN, slot), pl.ds(jnp.where(side == 0, slot, SLOTS - 1 - slot), 1), :]
         bias = bias[:, :half]
-        right = buf[m, slot, h]
+        left = buf[side, OWN].reshape(rows, buf.shape[4])
+        scores = (SCALE * LOG2E) * lax.dot_general(
+            left, buf[m, slot, h], NT, preferred_element_type=jnp.float32
+        ) + bias
+        sc[slot, side, h] = scores
         for r in range(2):
             part = pl.ds(r * half, half)
-            s = (SCALE * LOG2E) * lax.dot_general(
-                buf[side, OWN, r], right, NT, preferred_element_type=jnp.float32
-            ) + bias
-            sc[slot, side, h, part, :] = s
+            s = scores[r * half:(r + 1) * half]
             groups = [s[:, c:c + LANES] for c in range(0, half, LANES)]
             old = tops[side, part, :]
             top = functools.reduce(jnp.maximum, groups, old)
@@ -299,10 +300,19 @@
         for slot in pair:
             put(lbuf.at[slot], lbuf.at[slot], sibling, lsend.at[0], lrecv.at[slot]).wait_recv()
         for side in range(2):
-            for r in range(0, rows, half):
-                part = pl.ds(r, half)
-                terms = [product(weight(slot, side, part)[1], slot, side) for slot in pair]
-                grads[side][part, :] += terms[0] + terms[1]
+            ws = [
+                jnp.concatenate(
+                    [weight(slot, side, pl.ds(r, half))[1].astype(jnp.bfloat16) for r in range(0, rows, half)], axis=0
+                )
+                for slot in pair
+            ]
+            for n in range(0, buf.shape[4], rows):
+                cols = pl.ds(n, rows)
+                terms = [
+                    jnp.dot(w, buf[1 - side, slot, :, :, cols].reshape(rows, rows), preferred_element_type=jnp.float32)
+                    for w, slot in zip(ws, pair)
+                ]
+                grads[side][:, cols] += terms[0] + terms[1]
         return carry
 
     lax.fori_loop(0, RANGE, later, 0)

time: 135 us -> 134 us (level)
  no operation moved by 1% of the time
where the time goes in v5:
time: 134 us; the launch traced here: 132 us
  Pallas kernels  123 us (92%)
  local copies, waits for them, and re-layouts  6.64 us (5%)
    pallas_call x1, Pallas kernels, body(): pl.pallas_call(functools.partial(kernel, chips), out_shape=(jax.ShapeDtyp...  123 us
    unnamed x4, local copies, waits for them, and re-layouts  4.63 us

profile of v5, /device:TPU:0, one launch (start us, length us, event | category | flops | bytes accessed | tf_op | source)
XLA Modules:
  0.0 132.1 jit_solution(3650173561757942417)
XLA Ops:
  1.3 0.7 and_reduce_fusion
  2.1 0.7 broadcast_in_dim.18.bias_ref
  2.8 123.4 %shard_map.84 = (f32[512,1024]{1,0:T(8,128)}, f32[512,1024]{1,0:T(8,128)}, f32[2,8,512]{2,1,0:T(8,128)}) custom-call(bf16[512,1024]{1,0:T(8,128)(2,1)} %q_hbm.1, bf16[512,1024]{1,0:T(8,128)(2,1)} %p_hbm.1, f32[16,512]{1,0:T(8,128)} %broadcast_in_dim.18.bias_ref, s32[1,512]{1,0:T(1,128)} %pos_row.1), custom_call_target="tpu_custom_call" | custom-call | flops 19327352832 | bytes 6291456 | tf_op jit(solution)/shard_map/pallas_call | solution.py:366
  126.1 1.3 %slice_bitcast_fusion = (f32[1,512]{1,0:T(1,128)}, f32[1,512]{1,0:T(1,128)}) fusion(f32[2,8,512]{2,1,0:T(8,128)} %get-tuple-element.7), kind=kLoop, calls=%fused_computation.3 | loop fusion | bytes 8192 | tf_op jit(solution)/shard_map/squeeze | solution.py:399
  127.5 0.0 copy-start
  127.5 3.3 %copy.12 = f32[512,1024]{1,0:T(8,128)} copy(f32[512,1024]{1,0:T(8,128)} %get-tuple-element.18) | data formatting | bytes 4194304
  130.8 0.0 copy-done
  130.8 1.3 copy.13
  (4 shorter events, 0.0 us)
Async XLA Ops:
  127.5 3.3 %copy-start = (f32[512,1024]{1,0:T(8,128)S(1)}, f32[512,1024]{1,0:T(8,128)}, u32[]{:S(2)}) copy-start(f32[512,1024]{1,0:T(8,128)} %get-tuple-element.19) | copy-start | bytes 6291460

commit v6 on v5

--- a/solution.py
+++ b/solution.py
@@ -191,27 +191,23 @@
     lax.fori_loop(0, 4, own, 0)
     for o in others:
         bias_arrival(OWN - o).wait_recv()
-    lax.fori_loop(0, 4, beside, 0)
 
     def step(t, carry):
         @pl.when(t < 6)
         def _():
+            slot, m = pick(y_in, t)
+            arrival(slot, m, t % 2).wait_recv()
+
+            @pl.when(t < z_count())
+            def _():
+                z_send(t).start()
+
             slot, m = pick(x_in, t)
             arrival(slot, m, t % 2).wait_recv()
 
             @pl.when(t < 4)
             def _():
                 x_send(t + 2).start()
-
-            slot, m = pick(y_in, t)
-            arrival(slot, m, t % 2).wait_recv()
-
-            @pl.when(t < z_count())
-            def _():
-                z_send(t).start()
-
-            @pl.when(t < 4)
-            def _():
                 y_send(t + 2).start()
 
             for groups, n in ((x_in, 18), (y_in, 24)):
@@ -256,6 +252,11 @@
             return carry
 
         lax.fori_loop(0, 6, sub, 0)
+
+        @pl.when(t < 4)
+        def _():
+            beside(t, 0)
+
         return carry
 
     lax.fori_loop(0, 8, step, 0)

time: 134 us -> 132 us (0.985)
  Pallas kernels: 123 us -> 121 us
    pallas_call x1, Pallas kernels: 123 us -> 121 us  [body(): pl.pallas_call(functools.partial(kernel, chips), out_shape=(jax.ShapeDtyp...]
where the time goes in v6:
time: 132 us; the launch traced here: 130 us
  Pallas kernels  121 us (92%)
  local copies, waits for them, and re-layouts  6.64 us (5%)
    pallas_call x1, Pallas kernels, body(): pl.pallas_call(functools.partial(kernel, chips), out_shape=(jax.ShapeDtyp...  121 us
    unnamed x4, local copies, waits for them, and re-layouts  4.63 us

profile of v6, /device:TPU:0, one launch (start us, length us, event | category | flops | bytes accessed | tf_op | source)
XLA Modules:
  0.0 130.0 jit_solution(17608543798613443681)
XLA Ops:
  1.3 0.7 and_reduce_fusion
  2.1 0.7 broadcast_in_dim.18.bias_ref
  2.8 121.3 %shard_map.84 = (f32[512,1024]{1,0:T(8,128)}, f32[512,1024]{1,0:T(8,128)}, f32[2,8,512]{2,1,0:T(8,128)}) custom-call(bf16[512,1024]{1,0:T(8,128)(2,1)} %q_hbm.1, bf16[512,1024]{1,0:T(8,128)(2,1)} %p_hbm.1, f32[16,512]{1,0:T(8,128)} %broadcast_in_dim.18.bias_ref, s32[1,512]{1,0:T(1,128)} %pos_row.1), custom_call_target="tpu_custom_call" | custom-call | flops 19327352832 | bytes 6291456 | tf_op jit(solution)/shard_map/pallas_call | solution.py:367
  124.1 1.3 %slice_bitcast_fusion = (f32[1,512]{1,0:T(1,128)}, f32[1,512]{1,0:T(1,128)}) fusion(f32[2,8,512]{2,1,0:T(8,128)} %get-tuple-element.7), kind=kLoop, calls=%fused_computation.3 | loop fusion | bytes 8192 | tf_op jit(solution)/shard_map/squeeze | solution.py:400
  125.4 0.0 copy-start
  125.4 3.3 %copy.12 = f32[512,1024]{1,0:T(8,128)} copy(f32[512,1024]{1,0:T(8,128)} %get-tuple-element.18) | data formatting | bytes 4194304
  128.7 0.0 copy-done
  128.7 1.3 %copy.13 = f32[512,1024]{1,0:T(8,128)} copy(f32[512,1024]{1,0:T(8,128)S(1)} %copy-done) | data formatting | bytes 4194304
  (4 shorter events, 0.0 us)
Async XLA Ops:
  125.4 3.3 %copy-start = (f32[512,1024]{1,0:T(8,128)S(1)}, f32[512,1024]{1,0:T(8,128)}, u32[]{:S(2)}) copy-start(f32[512,1024]{1,0:T(8,128)} %get-tuple-element.19) | copy-start | bytes 6291460
